TPU v7x, 32 devices: a whole 2x2x4 slice. The times are simulated.
32 devices in a mesh: group: 2 (over core), seq: 4 (over z), tensor: 4 (over y, x).
Axes of the slice: x: 2, y: 2, z: 4, core: 2. Of those that a mesh axis runs over, the one named last changes fastest.
Arguments:
- prompt_hidden: bfloat16 [12288, 12288], P(('group', 'seq'), 'tensor')
- decode_hidden: bfloat16 [2, 32, 12288], P(None, ('group', 'seq'), 'tensor')
- norm_gain: bfloat16 [12288], P('tensor'), may hold values from 0.099609375 to 1.8984375
- kv_weight: bfloat16 [12288, 2048], P('tensor'), may hold values from -0.0546875 to 0.0546875
- kv_cache: bfloat16 [32, 8, 1024, 256], P(('group', 'seq'), None, 'tensor'), as said below
- queries: bfloat16 [2, 32, 12288], P(None, ('group', 'seq')), as said below
- lengths: int32 [32], replicated, may hold values from 2 to 254, as said below
- prompt_row: int32 [16], replicated, may hold values from 0 to 31, as said below
Outputs:
- decode_out: bfloat16 [2, 32, 12288], P(None, ('group', 'seq'), 'tensor')
Inputs may be any that keep to these rules, and one draw needn't show every extreme that they name: `lengths`: one row has exactly 254 and one row exactly 2. `prompt_row`: no two prompts share a row. `kv_cache`: keys already rotated to their positions. queries already rotated to their positions.
All inputs are finite; a program needn't handle non-finite values.
Results may differ from a plain program's by a relative error of at most 0.02.
Values may be sent and summed in bfloat16 or wider, within the bound.
A program may use at most 128 MiB of HBM per device.

v0:
```python
import math

import jax
import jax.numpy as jnp
from jax import lax
from jax.sharding import PartitionSpec as P

D = 12288
PLEN = 768


epsilon = 1e-05
rope_base = 1000000.0
very_negative = -1e30


def combined_all(shard, axis, join):
    gathered = jax.tree.map(
        lambda a, kind: lax.all_gather(a.astype(kind), axis),
        shard,
        (jnp.bfloat16, jnp.bfloat16, jnp.bfloat16),
    )

    def take(source):
        return jax.tree.map(
            lambda a, own: lax.dynamic_index_in_dim(a, source, 0, False).astype(own.dtype),
            gathered,
            shard,
        )

    return lax.fori_loop(
        1, lax.axis_size(axis), lambda source, state: join(state, take(source)), take(0)
    )


def rotate(values, positions):
    halfway = values.shape[-1] // 2
    exponents = jnp.arange(halfway, dtype=jnp.float32) * (-2.0 / values.shape[-1])
    frequency = jnp.power(rope_base, exponents)
    angles = positions.astype(jnp.float32)[..., None] * frequency
    cosine = jnp.cos(angles)
    sine_part = jnp.sin(angles)
    leading = values[..., :halfway]
    trailing = values[..., halfway:]
    return jnp.concatenate(
        [leading * cosine - trailing * sine_part, trailing * cosine + leading * sine_part], -1
    )


def owner_rows(tokens, prompt_row):
    matches = (tokens // PLEN)[:, None] == jnp.arange(prompt_row.shape[0], dtype=jnp.int32)[None, :]
    return jnp.sum(jnp.where(matches, prompt_row[None, :], 0), axis=1)


def token_positions(tokens, owners, lengths):
    matches = owners[:, None] == jnp.arange(lengths.shape[0], dtype=jnp.int32)[None, :]
    return jnp.sum(jnp.where(matches, lengths[None, :], 0), axis=1) + tokens % PLEN


def absorb(carried, scores, mask_table, mix_values):
    old_top, old_total, old_mixed = carried
    masked = jnp.where(mask_table, scores, very_negative)
    new_top = jnp.maximum(old_top, jnp.max(masked, axis=-1))
    weights = jnp.where(mask_table, jnp.exp(masked - new_top[..., None]), 0.0)
    rescale = jnp.exp(old_top - new_top)
    new_total = old_total * rescale + jnp.sum(weights, axis=-1)
    new_mixed = old_mixed * rescale[..., None] + mix_values(weights.astype(jnp.bfloat16))
    return (new_top, new_total, new_mixed)


def join_states(leading, trailing):
    largest = jnp.maximum(leading[0], trailing[0])
    left_factor = jnp.exp(leading[0] - largest)
    right_factor = jnp.exp(trailing[0] - largest)
    return (
        largest,
        leading[1] * left_factor + trailing[1] * right_factor,
        leading[2] * left_factor[..., None] + trailing[2] * right_factor[..., None],
    )


def per_device(
    prompt_hidden, decode_hidden, norm_gain, kv_weight, kv_cache, queries, lengths, prompt_row
):
    tensor_count = lax.axis_size("tensor")
    tensor_rank = lax.axis_index("tensor")
    shard_rank = lax.axis_index(("group", "seq"))
    token_count = prompt_hidden.shape[0]
    slice_rows = token_count // tensor_count
    steps_count = queries.shape[0]
    row_count = queries.shape[1]
    kv_heads = kv_cache.shape[1]
    cache_rows = kv_cache.shape[2]
    head_size = kv_cache.shape[3] // 2
    query_heads = queries.shape[2] // head_size
    group_size = query_heads // kv_heads
    score_scale = 1.0 / math.sqrt(head_size)
    gain_wide = norm_gain.astype(jnp.float32)
    prompt_wide = prompt_hidden.astype(jnp.float32)
    prompt_square = jnp.sum(prompt_wide * prompt_wide, axis=1)
    prompt_weighted = (prompt_wide * gain_wide).astype(jnp.bfloat16)
    decode_wide = decode_hidden.astype(jnp.float32)
    decode_square = jnp.sum(decode_wide * decode_wide, axis=2)
    decode_weighted = (decode_wide * gain_wide).astype(jnp.bfloat16)
    decode_terms = jnp.einsum(
        "srk,kc->src", decode_weighted, kv_weight, preferred_element_type=jnp.float32
    )
    prompt_square, decode_square, decode_terms = (
        lax.psum(prompt_square.astype(jnp.bfloat16), "tensor").astype(jnp.float32),
        lax.psum(decode_square.astype(jnp.bfloat16), "tensor").astype(jnp.float32),
        lax.psum(decode_terms.astype(jnp.bfloat16), "tensor").astype(jnp.float32),
    )
    my_rows = shard_rank * row_count + jnp.arange(row_count, dtype=jnp.int32)
    my_lengths = lax.dynamic_slice_in_dim(lengths, shard_rank * row_count, row_count, 0)
    is_new = jnp.any(prompt_row[None, :] == my_rows[:, None], axis=1)
    step_ids = jnp.arange(steps_count, dtype=jnp.int32)
    step_pos = my_lengths[None, :] + PLEN * is_new.astype(jnp.int32)[None, :] + step_ids[:, None]
    decode_scaled = decode_terms * lax.rsqrt(decode_square / D + epsilon)[..., None]
    decode_heads = decode_scaled.reshape(steps_count, row_count, kv_heads, 2, head_size)
    step_keys = rotate(decode_heads[:, :, :, 0], step_pos[:, :, None]).astype(jnp.bfloat16)
    step_values = decode_heads[:, :, :, 1].astype(jnp.bfloat16)
    full_terms = jnp.dot(prompt_weighted, kv_weight, preferred_element_type=jnp.float32)
    column_part = lax.psum_scatter(
        full_terms.astype(jnp.bfloat16), "tensor", scatter_dimension=1, tiled=True
    ).astype(jnp.float32)
    all_tokens = shard_rank * token_count + jnp.arange(token_count, dtype=jnp.int32)
    all_owners = owner_rows(all_tokens, prompt_row)
    positions = token_positions(all_tokens, all_owners, lengths)
    scaled = column_part * lax.rsqrt(prompt_square / D + epsilon)[:, None]
    pieces = column_part.shape[1] // head_size
    halves = scaled.reshape(token_count, pieces, head_size)
    rotated = rotate(halves, positions[:, None])
    half_index = tensor_rank * pieces + jnp.arange(pieces, dtype=jnp.int32)
    chosen = jnp.where((half_index % 2 == 0)[None, :, None], rotated, halves)
    column_block = chosen.reshape(token_count, pieces * head_size).astype(jnp.bfloat16)
    handed = lax.all_to_all(column_block, "tensor", split_axis=0, concat_axis=1, tiled=True)
    query_blocks = queries.reshape(steps_count, row_count, kv_heads, group_size, head_size)
    cache_keys = kv_cache[..., :head_size]
    cache_values = kv_cache[..., head_size:]
    cache_pos = tensor_rank * cache_rows + jnp.arange(cache_rows, dtype=jnp.int32)
    cache_mask = (cache_pos[None, :] < my_lengths[:, None])[None, :, None, None, :]
    cache_scores = (
        jnp.einsum(
            "srgqd,rgpd->srgqp", query_blocks, cache_keys, preferred_element_type=jnp.float32
        )
        * score_scale
    )

    def mix_cache(rounded):
        return jnp.einsum(
            "srgqp,rgpd->srgqd", rounded, cache_values, preferred_element_type=jnp.float32
        )

    state_shape = (steps_count, row_count, kv_heads, group_size)
    start_state = (
        jnp.full(state_shape, very_negative, jnp.float32),
        jnp.zeros(state_shape, jnp.float32),
        jnp.zeros(state_shape + (head_size,), jnp.float32),
    )
    state = absorb(start_state, cache_scores, cache_mask, mix_cache)
    step_owner = step_pos // cache_rows == tensor_rank
    causal = step_ids[None, :] <= step_ids[:, None]
    step_mask = (causal[:, None, :] & jnp.transpose(step_owner)[None, :, :])[:, :, None, None, :]
    step_scores = (
        jnp.einsum("srgqd,trgd->srgqt", query_blocks, step_keys, preferred_element_type=jnp.float32)
        * score_scale
    )

    def mix_steps(rounded):
        return jnp.einsum(
            "srgqt,trgd->srgqd", rounded, step_values, preferred_element_type=jnp.float32
        )

    state = absorb(state, step_scores, step_mask, mix_steps)
    portion = lax.all_gather(handed, ("group", "seq"), axis=0, tiled=True)
    portion_rows = portion.shape[0]
    whole_index = jnp.arange(portion_rows, dtype=jnp.int32)
    tokens = (
        whole_index // slice_rows * token_count
        + tensor_rank * slice_rows
        + whole_index % slice_rows
    )
    portion_owners = owner_rows(tokens, prompt_row)
    portion_heads = portion.reshape(portion_rows, kv_heads, 2, head_size)
    portion_mask = (portion_owners[None, :] == my_rows[:, None])[None, :, None, None, :]
    portion_scores = (
        jnp.einsum(
            "srgqd,ngd->srgqn",
            query_blocks,
            portion_heads[:, :, 0],
            preferred_element_type=jnp.float32,
        )
        * score_scale
    )

    def mix_portion(rounded):
        return jnp.einsum(
            "srgqn,ngd->srgqd", rounded, portion_heads[:, :, 1], preferred_element_type=jnp.float32
        )

    state = absorb(state, portion_scores, portion_mask, mix_portion)
    top_part, total_part, mixed_part = state
    local_heads = query_heads // tensor_count
    top_part, total_part, mixed_part = combined_all(
        (top_part, total_part, mixed_part), "tensor", join_states
    )
    result_all = (mixed_part / total_part[..., None]).reshape(
        steps_count, row_count, query_heads * head_size
    )
    result = lax.dynamic_slice_in_dim(
        result_all, tensor_rank * local_heads * head_size, local_heads * head_size, 2
    )
    return result.astype(jnp.bfloat16)


def solution(mesh):
    return jax.shard_map(
        per_device,
        mesh=mesh,
        in_specs=(
            P(("group", "seq"), "tensor"),
            P(None, ("group", "seq"), "tensor"),
            P("tensor"),
            P("tensor", None),
            P(("group", "seq"), None, "tensor", None),
            P(None, ("group", "seq"), None),
            P(),
            P(),
        ),
        out_specs=P(None, ("group", "seq"), "tensor"),
        check_vma=False,
    )
```

profile of v0, /device:TPU:0, one launch (start us, length us, event | category | flops | bytes accessed | tf_op | source)
XLA Modules:
  0.0 340.9 jit_solution(9837533422658987263)
XLA Ops:
  6.5 0.7 convert_element_type.159
  7.2 26.2 %fusion.12 = bf16[1536,2048]{1,0:T(8,128)(2,1)} fusion(bf16[3072,2048]{1,0:T(8,128)(2,1)} %param.13, bf16[1536,3072]{1,0:T(8,128)(2,1)} %param.10, f32[3072]{0:T(1024)S(1)} %convert_element_type.159), kind=kOutput, calls=%fused_computation.23 | convolution fusion | flops 19344654336 | bytes 28323840 | tf_op jit(solution)/shard_map/dot_general | solution.py:122
  33.5 0.7 copy-done.2
  34.2 0.1 fusion.66
  34.3 5.6 %fusion.4 = bf16[1536]{0:T(1024)(128)(2,1)S(1)} fusion(bf16[1536,3072]{1,0:T(8,128)(2,1)} %param.10), kind=kLoop, calls=%fused_computation.13 | loop fusion | flops 14154240 | bytes 9440256 | tf_op jit(solution)/shard_map/reduce_sum | solution.py:100
  39.9 7.5 %fusion.20 = bf16[2,4,2048]{2,1,0:T(4,128)(2,1)S(1)} fusion(bf16[3072,2048]{1,0:T(8,128)(2,1)} %param.13, bf16[2,4,3072]{2,1,0:T(4,128)(2,1)S(1)} %copy-done.2, f32[3072]{0:T(1024)S(1)} %convert_element_type.159), kind=kOutput, calls=%fused_computation.36 | convolution fusion | flops 100753408 | bytes 12677120 | tf_op jit(solution)/shard_map/srk,kc->src/dot_general | solution.py:105
  47.4 19.6 %all-reduce = (bf16[1536]{0:T(1024)(128)(2,1)S(1)}, bf16[2,4,2048]{2,1,0:T(4,128)(2,1)S(1)}, bf16[2,4]{1,0:T(2,128)(2,1)S(1)}) all-reduce(bf16[1536]{0:T(1024)(128)(2,1)S(1)} %fusion.4, bf16[2,4,2048]{2,1,0:T(4,128)(2,1)S(1)} %fusion.20, bf16[2,4]{1,0:T(2,128)(2,1)S(1)} %fusion.66), channel_id=1, replica_groups=mesh['group'=2,'seq'=4,'tensor'=4] {'tensor'}, use_global_device_ids=true, to_apply=%region_9.10 | all-reduce | flops 17928 | bytes 71712 | tf_op jit(solution)/shard_map/psum | solution.py:109
  67.1 0.1 select_reduce_fusion.2
  67.3 0.1 select_reduce_fusion
  67.5 4.3 %multiply_cosine_fusion = (f32[1536,64]{1,0:T(8,128)}, f32[1536,64]{1,0:T(8,128)}) fusion(f32[64]{0:T(128)S(1)} %multiply_power_fusion, f32[1536]{0:T(1024)S(1)} %fusion.95), kind=kLoop, calls=%fused_computation.56 | loop fusion | flops 98304 | bytes 792832 | tf_op jit(solution)/shard_map/cos | solution.py:41
  71.8 36.2 %reduce-scatter.2.cloned.1.call-done = bf16[1536,512]{1,0:T(8,128)(2,1)} async-done(((bf16[1536,2048]{1,0:T(8,128)(2,1)}), bf16[1536,512]{1,0:T(8,128)(2,1)}) %reduce-scatter.2.cloned.1.call-update) | async-done | bytes 1572880 | tf_op jit(solution)/shard_map/reduce_scatter | solution.py:123
  108.0 3.4 convert_multiply_fusion.4
  111.3 3.1 reshape.449
  114.5 3.4 multiply_subtract_fusion
  117.8 2.2 pad_maximum_fusion
  120.0 0.5 fusion.18
  120.6 0.9 copy.77
  121.5 23.2 %all_to_all.19 = bf16[4,384,512]{1,2,0:T(8,128)(2,1)} all-to-all(bf16[4,384,512]{1,2,0:T(8,128)(2,1)S(1)} %copy.77), channel_id=1, replica_groups=mesh['group'=2,'seq'=4,'tensor'=4] {'tensor'}, dimensions={0} | all-to-all | bytes 3145728 | tf_op jit(solution)/shard_map/all_to_all | solution.py:136
  145.0 0.2 reshape.447
  145.3 0.2 compare_reduce_fusion
  145.5 0.1 select_reduce_fusion.1
  145.9 0.1 multiply_cosine_fusion.1
  146.1 0.1 subtract_convert_fusion
  146.2 0.8 fusion.114
  147.0 2.5 fusion.115
  149.6 111.4 %all-gather.3.cloned.1.call-done = bf16[3072,2048]{0,1:T(8,128)(2,1)} async-done(((bf16[384,2048]{0,1:T(8,128)(2,1)}), bf16[3072,2048]{0,1:T(8,128)(2,1)}) %all-gather.3.cloned.1.call-update) | async-done | bytes 12582928 | tf_op jit(solution)/shard_map/all_gather | solution.py:175
  261.0 4.6 %fusion.16 = f32[8,3072,2,4,12]{1,4,3,2,0:T(8,128)S(1)} fusion(bf16[3072,8,2,128]{0,3,2,1:T(8,128)(2,1)} %bitcast.188, bf16[2,4,8,12,128]{4,3,2,1,0:T(8,128)(2,1)S(1)} %reshape.447), kind=kOutput, calls=%fused_computation.27 | convolution fusion | flops 603979776 | bytes 15925248 | tf_op jit(solution)/shard_map/srgqd,ngd->srgqn/dot_general | solution.py:187
  265.6 4.5 %copy-done = f32[8,3072,2,4,12]{1,4,3,2,0:T(8,128)} copy-done((f32[8,3072,2,4,12]{1,4,3,2,0:T(8,128)}, f32[8,3072,2,4,12]{1,4,3,2,0:T(8,128)S(1)}, u32[]{:S(2)}) %copy-start) | copy-done | bytes 9437208
  270.0 6.3 %fusion.19 = f32[2,4,8,12]{2,3,1,0:T(8,128)S(1)} fusion(f32[8,3072,2,4,12]{1,4,3,2,0:T(8,128)S(1)} %fusion.16, pred[4,3072]{1,0:T(4,128)(4,1)S(1)} %broadcast_compare_fusion), kind=kLoop, calls=%fused_computation.35 | loop fusion | flops 7077120 | bytes 9452544 | tf_op jit(solution)/shard_map/reduce_max | solution.py:63
  276.3 0.1 copy.82
  276.5 8.4 %all_gather.18 = bf16[4,2,4,8,12]{4,3,2,1,0:T(8,128)(2,1)S(1)} all-gather(bf16[1,2,4,8,12]{4,3,2,1,0:T(8,128)(2,1)S(1)} %copy.83), channel_id=1, replica_groups=mesh['group'=2,'seq'=4,'tensor'=4] {'tensor'}, dimensions={0}, use_global_device_ids=true | all-gather | bytes 7680 | tf_op jit(solution)/shard_map/all_gather | solution.py:19
  285.0 0.2 fusion.105
  285.2 0.1 copy.85
  285.3 12.0 %fusion.10 = (bf16[2,4,8,12,3072]{4,2,3,1,0:T(8,128)(2,1)S(1)}, f32[2,4,8,12]{2,3,1,0:T(8,128)S(1)}) fusion(f32[2,4,8,12]{2,3,1,0:T(8,128)S(1)} %copy.85, pred[4,3072]{1,0:T(4,128)(4,1)S(1)} %broadcast_compare_fusion, f32[8,3072,2,4,12]{1,4,3,2,0:T(8,128)} %copy-done), kind=kLoop, calls=%fused_computation.21 | loop fusion | flops 14155008 | bytes 14174208 | tf_op jit(solution)/shard_map/convert_element_type | solution.py:67
  297.4 9.7 %fusion.50 = f32[2,4,8,12,128]{4,3,0,2,1:T(8,128)S(1)} fusion(bf16[2,4,8,12,3072]{4,2,3,1,0:T(8,128)(2,1)S(1)} %get-tuple-element.245, bf16[3072,8,2,128]{0,3,2,1:T(8,128)(2,1)} %bitcast.189), kind=kOutput, calls=%fused_computation.53 | convolution fusion | flops 603979776 | bytes 11403264 | tf_op jit(solution)/shard_map/srgqn,ngd->srgqd/dot_general | solution.py:197
  307.1 0.1 copy.87
  307.2 0.4 fusion.57
  307.6 0.1 fusion.69
  307.7 8.2 %all_gather.19 = bf16[4,2,4,8,12]{4,3,2,1,0:T(8,128)(2,1)S(1)} all-gather(bf16[1,2,4,8,12]{4,3,2,1,0:T(8,128)(2,1)S(1)} %copy.88), channel_id=1, replica_groups=mesh['group'=2,'seq'=4,'tensor'=4] {'tensor'}, dimensions={0}, use_global_device_ids=true | all-gather | bytes 7680 | tf_op jit(solution)/shard_map/all_gather | solution.py:19
  315.9 2.2 fusion.45
  318.1 0.6 fusion.53
  318.7 12.6 %all-gather = bf16[8,4,8,12,128]{4,3,0,2,1:T(8,128)(2,1)S(1)} all-gather(bf16[2,4,8,12,128]{4,3,0,2,1:T(8,128)(2,1)S(1)} %fusion.53), channel_id=2, replica_groups=mesh['group'=2,'seq'=4,'tensor'=4] {'tensor'}, dimensions={0}, use_global_device_ids=true | all-gather | bytes 983040 | tf_op jit(solution)/shard_map/all_gather | solution.py:19
  331.4 1.7 while.19
  331.5 0.5 fusion.120
  332.0 0.5 fusion.120
  332.6 0.5 fusion.120
  333.1 0.2 broadcast_divide_fusion
  333.4 0.6 dynamic-slice_convert_fusion
  (49 shorter events, 1.4 us)
Async XLA Ops:
  6.5 101.4 %reduce-scatter.2.cloned.1.call-start = ((), (), s32[]{:S(2)}) async-start(), calls=%async_computation.2 | async-start | bytes 7864320 | tf_op jit(solution)/shard_map/reduce_scatter | solution.py:123
  33.4 0.8 copy-start.2
  33.4 227.6 %all-gather.3.cloned.1.call-start = ((), (), s32[]{:S(2)}) async-start(), calls=%async_computation.3 | async-start | bytes 14155776 | tf_op jit(solution)/shard_map/all_gather | solution.py:175
  39.9 27.2 %copy-start.4 = (s32[16]{0:T(128)S(1)}, s32[16]{0:T(128)}, u32[]{:S(2)}) copy-start(s32[16]{0:T(128)} %param.17) | copy-start | bytes 196
  39.9 27.3 %copy-start.5 = (s32[32]{0:T(128)S(1)}, s32[32]{0:T(128)}, u32[]{:S(2)}) copy-start(s32[32]{0:T(128)} %param.16) | copy-start | bytes 388
  117.8 2.2 copy-start.1
  120.6 24.4 %copy-start.3 = (bf16[2,4,12288]{2,1,0:T(4,128)(2,1)S(1)}, bf16[2,4,12288]{2,1,0:T(4,128)(2,1)}, u32[]{:S(2)}) copy-start(bf16[2,4,12288]{2,1,0:T(4,128)(2,1)} %param.15) | copy-start | bytes 589828
  265.6 4.5 %copy-start = (f32[8,3072,2,4,12]{1,4,3,2,0:T(8,128)}, f32[8,3072,2,4,12]{1,4,3,2,0:T(8,128)S(1)}, u32[]{:S(2)}) copy-start(f32[8,3072,2,4,12]{1,4,3,2,0:T(8,128)S(1)} %fusion.16) | copy-start | bytes 28311556
Sparse Core Ops, SparseCore 0:
  33.6 74.3 reduce-scatter.1
  144.8 116.1 all-gather.2
where the time goes:
time: 341 us
  waiting for transfers between devices  148 us (43%)
  blocking collectives  72.1 us (21%)
  matrix products  54 us (16%)
  other arithmetic  42.4 us (12%)
  between operations  13.8 us (4%)
  local copies, waits for them, and re-layouts  10.8 us (3%)
    all_gather x1, waiting for transfers between devices, per_device(): portion = lax.all_gather(handed, ('group', 'seq'), axis=0, tiled=True)  111 us
    reduce_scatter x1, waiting for transfers between devices, per_device(): lax.psum_scatter(full_terms.astype(jnp.bfloat16), 'tensor', scatter_dimen...  36.2 us
    all_gather x3, blocking collectives, combined_all(): lax.all_gather(a.astype(kind), axis)  29.3 us
    dot_general x1, matrix products, per_device(): jnp.dot(prompt_weighted, kv_weight, preferred_element_type=jnp.float32)  26.2 us
    all_to_all x1, blocking collectives, per_device(): lax.all_to_all(column_block, 'tensor', split_axis=0, concat_axis=1, tiled...  23.2 us
    psum x1, blocking collectives, per_device(): lax.psum(prompt_square.astype(jnp.bfloat16), 'tensor').astype(jnp.float32)  19.6 us
    convert_element_type x1, other arithmetic, absorb(): weights.astype(jnp.bfloat16)  12 us
    dot_general x1, matrix products, mix_portion(): jnp.einsum('srgqn,ngd->srgqd', rounded, portion_heads[:, :, 1], preferred...  9.69 us
  transfers between devices with their start and end apart: 2, of which 2 were waited for; matrix products, arithmetic and copies ran while one was open for 7% of the time, Pallas kernels for 0%

commit v1 on v0

v1 whole, which is shorter than its diff:
```python
import math

import jax
import jax.numpy as jnp
from jax import lax
from jax.sharding import PartitionSpec as P

D = 12288
PLEN = 768


epsilon = 1e-05
rope_base = 1000000.0
very_negative = -1e30


def angle_parts(positions, head_size):
    halfway = head_size // 2
    exponents = jnp.arange(halfway, dtype=jnp.float32) * (-2.0 / head_size)
    frequency = jnp.power(rope_base, exponents)
    angles = positions.astype(jnp.float32)[..., None] * frequency
    return jnp.cos(angles), jnp.sin(angles)


def rotate(values, cosine, sine_part):
    halfway = values.shape[-1] // 2
    leading = values[..., :halfway]
    trailing = values[..., halfway:]
    return jnp.concatenate(
        [leading * cosine - trailing * sine_part, trailing * cosine + leading * sine_part], -1
    )


def per_device(
    prompt_hidden, decode_hidden, norm_gain, kv_weight, kv_cache, queries, lengths, prompt_row
):
    shards = ("group", "seq")
    tensor_count = lax.axis_size("tensor")
    tensor_rank = lax.axis_index("tensor")
    shard_rank = lax.axis_index(shards)
    token_count, features = prompt_hidden.shape
    steps_count, row_count, query_width = queries.shape
    kv_heads = kv_cache.shape[1]
    cache_rows = kv_cache.shape[2]
    head_size = kv_cache.shape[3] // 2
    query_heads = query_width // head_size
    group_size = query_heads // kv_heads
    local_heads = query_heads // tensor_count
    local_prompts = token_count // PLEN
    score_scale = 1.0 / math.sqrt(head_size)
    row_total = lengths.shape[0]

    my_owners = lax.dynamic_slice_in_dim(
        prompt_row, shard_rank * local_prompts, local_prompts, 0
    )
    width = query_width // tensor_count
    my_queries = lax.dynamic_slice_in_dim(queries, tensor_rank * width, width, 2)
    query_rows = lax.all_gather(my_queries, shards, axis=1, tiled=True)
    owner_queries = jnp.take(query_rows, my_owners, axis=1)
    owner_queries = lax.all_gather(owner_queries, "tensor", axis=2, tiled=True)
    owner_queries = owner_queries.reshape(
        steps_count, local_prompts, kv_heads, group_size, head_size
    )

    gain_wide = norm_gain.astype(jnp.float32)
    prompt_wide = prompt_hidden.astype(jnp.float32)
    prompt_square = jnp.sum(prompt_wide * prompt_wide, axis=1)
    prompt_weighted = (prompt_wide * gain_wide).astype(jnp.bfloat16)
    decode_wide = decode_hidden.astype(jnp.float32)
    decode_square = jnp.sum(decode_wide * decode_wide, axis=2)
    decode_weighted = (decode_wide * gain_wide).astype(jnp.bfloat16)
    decode_terms = jnp.einsum(
        "srk,kc->src", decode_weighted, kv_weight, preferred_element_type=jnp.float32
    )

    my_rows = shard_rank * row_count + jnp.arange(row_count, dtype=jnp.int32)
    my_lengths = lax.dynamic_slice_in_dim(lengths, shard_rank * row_count, row_count, 0)
    query_blocks = queries.reshape(steps_count, row_count, kv_heads, group_size, head_size)
    cache_pos = tensor_rank * cache_rows + jnp.arange(cache_rows, dtype=jnp.int32)
    cache_mask = (cache_pos[None, :] < my_lengths[:, None])[:, None, None, None, :]
    cache_scores = (
        jnp.einsum(
            "srgqd,rgpd->rgsqp",
            query_blocks,
            kv_cache[..., :head_size],
            preferred_element_type=jnp.float32,
        )
        * score_scale
    )
    cache_scores = jnp.where(cache_mask, cache_scores, very_negative)
    cache_top = jnp.max(cache_scores, axis=-1)
    cache_top = lax.pmax(cache_top, "tensor")
    cache_weights = jnp.where(cache_mask, jnp.exp(cache_scores - cache_top[..., None]), 0.0)
    cache_total = jnp.sum(cache_weights, axis=-1)
    cache_mixed = jnp.einsum(
        "rgsqp,rgpd->gqsrd",
        cache_weights.astype(jnp.bfloat16),
        kv_cache[..., head_size:],
        preferred_element_type=jnp.float32,
    ).reshape(query_heads, steps_count, row_count, head_size)
    cache_mixed = lax.psum_scatter(cache_mixed, "tensor", scatter_dimension=0, tiled=True)

    prompt_square, decode_square, decode_terms, cache_total = lax.psum(
        (prompt_square, decode_square, decode_terms, cache_total), "tensor"
    )

    weight_heads = kv_weight.reshape(features, kv_heads, 2, head_size)
    positions = (
        jnp.take(lengths, my_owners)[:, None] + jnp.arange(PLEN, dtype=jnp.int32)[None, :]
    )
    cosine, sine_part = angle_parts(positions, head_size)
    key_part = jnp.dot(
        prompt_weighted,
        weight_heads[:, :, 0].reshape(features, kv_heads * head_size),
        preferred_element_type=jnp.float32,
    ).reshape(local_prompts, PLEN, kv_heads, head_size)
    key_part = rotate(key_part, cosine[:, :, None], sine_part[:, :, None]).astype(jnp.bfloat16)
    scores = jnp.einsum(
        "spgqd,pngd->pgsqn", owner_queries, key_part, preferred_element_type=jnp.float32
    )
    scores = lax.psum(scores, "tensor")

    value_part = jnp.dot(
        prompt_weighted,
        weight_heads[:, :, 1].reshape(features, kv_heads * head_size),
        preferred_element_type=jnp.float32,
    ).astype(jnp.bfloat16)
    value_part = value_part.reshape(local_prompts, PLEN, kv_heads, head_size)

    factor = lax.rsqrt(prompt_square / D + epsilon).reshape(local_prompts, 1, 1, 1, PLEN)
    scores = scores * (factor * score_scale)
    prompt_top = jnp.max(scores, axis=-1)
    weights = jnp.exp(scores - prompt_top[..., None])
    prompt_total = jnp.sum(weights, axis=-1)
    prompt_log = prompt_top + jnp.log(prompt_total)
    mixed = jnp.einsum(
        "pgsqn,pngd->gqspd",
        (weights * factor).astype(jnp.bfloat16),
        value_part,
        preferred_element_type=jnp.float32,
    )
    totals = jnp.transpose(prompt_total, (1, 3, 2, 0))
    mixed = (mixed / totals[..., None]).reshape(
        query_heads, steps_count, local_prompts, head_size
    )
    mixed = lax.psum_scatter(mixed, "tensor", scatter_dimension=0, tiled=True)
    first_head = tensor_rank * local_heads
    prompt_log = jnp.transpose(prompt_log, (1, 3, 2, 0)).reshape(
        query_heads, steps_count, local_prompts
    )
    prompt_log = lax.dynamic_slice_in_dim(prompt_log, first_head, local_heads, 0)
    log_all = lax.all_gather(prompt_log, shards, axis=2, tiled=True)
    mixed_all = lax.all_gather(mixed.astype(jnp.bfloat16), shards, axis=2, tiled=True)

    owned = prompt_row[None, :] == my_rows[:, None]
    is_new = jnp.any(owned, axis=1)
    prompt_of_row = jnp.argmax(owned, axis=1)
    row_log = jnp.take(log_all, prompt_of_row, axis=2)
    row_log = jnp.where(is_new[None, None, :], row_log, very_negative)
    row_mixed = jnp.take(mixed_all, prompt_of_row, axis=2).astype(jnp.float32)
    row_mixed = jnp.where(is_new[None, None, :, None], row_mixed, 0.0)

    step_ids = jnp.arange(steps_count, dtype=jnp.int32)
    step_pos = my_lengths[None, :] + PLEN * is_new.astype(jnp.int32)[None, :] + step_ids[:, None]
    decode_scaled = decode_terms * lax.rsqrt(decode_square / D + epsilon)[..., None]
    decode_heads = decode_scaled.reshape(steps_count, row_count, kv_heads, 2, head_size)
    step_cosine, step_sine = angle_parts(step_pos, head_size)
    step_keys = rotate(
        decode_heads[:, :, :, 0], step_cosine[:, :, None], step_sine[:, :, None]
    ).astype(jnp.bfloat16)
    step_values = decode_heads[:, :, :, 1].astype(jnp.bfloat16)
    step_scores = (
        jnp.einsum(
            "srgqd,trgd->gqsrt", query_blocks, step_keys, preferred_element_type=jnp.float32
        )
        * score_scale
    )
    causal = step_ids[None, :] <= step_ids[:, None]
    step_mask = causal[None, None, :, None, :]
    step_scores = jnp.where(step_mask, step_scores, very_negative)
    step_top = jnp.max(step_scores, axis=-1)
    step_weights = jnp.where(step_mask, jnp.exp(step_scores - step_top[..., None]), 0.0)
    step_total = jnp.sum(step_weights, axis=-1)
    step_mixed = jnp.einsum(
        "gqsrt,trgd->gqsrd",
        step_weights.astype(jnp.bfloat16),
        step_values,
        preferred_element_type=jnp.float32,
    )

    def own(array):
        flat = array.reshape((query_heads,) + array.shape[2:])
        return lax.dynamic_slice_in_dim(flat, first_head, local_heads, 0)

    step_top, step_total, step_mixed = own(step_top), own(step_total), own(step_mixed)
    cache_top = own(jnp.transpose(cache_top, (1, 3, 2, 0)))
    cache_total = own(jnp.transpose(cache_total, (1, 3, 2, 0)))

    top = jnp.maximum(jnp.maximum(step_top, cache_top), row_log)
    step_factor = jnp.exp(step_top - top)
    cache_factor = jnp.exp(cache_top - top)
    row_factor = jnp.exp(row_log - top)
    total = step_total * step_factor + cache_total * cache_factor + row_factor
    result = (
        step_mixed * step_factor[..., None]
        + cache_mixed * cache_factor[..., None]
        + row_mixed * row_factor[..., None]
    ) / total[..., None]
    result = jnp.transpose(result, (1, 2, 0, 3)).reshape(
        steps_count, row_count, local_heads * head_size
    )
    return result.astype(jnp.bfloat16)


def solution(mesh):
    return jax.shard_map(
        per_device,
        mesh=mesh,
        in_specs=(
            P(("group", "seq"), "tensor"),
            P(None, ("group", "seq"), "tensor"),
            P("tensor"),
            P("tensor", None),
            P(("group", "seq"), None, "tensor", None),
            P(None, ("group", "seq"), None),
            P(),
            P(),
        ),
        out_specs=P(None, ("group", "seq"), "tensor"),
        check_vma=False,
    )
```

time: 341 us -> 233 us (0.68)
  waiting for transfers between devices: 148 us -> 2.5 us
  blocking collectives: 72.1 us -> 113 us
  local copies, waits for them, and re-layouts: 10.8 us -> 32.9 us
  other arithmetic: 42.4 us -> 26.3 us
  matrix products: 54 us -> 43.7 us
    all_gather x1 -> x0, waiting for transfers between devices: 111 us -> none  [per_device(): portion = lax.all_gather(handed, ('group', 'seq'), axis=0, tiled=True)]
    all_gather x3 -> x4, blocking collectives: 29.3 us -> 82.3 us  [the longest x1 27.6 us: per_device(): query_rows = lax.all_gather(my_queries, shards, axis=1, tiled=True)]
    reduce_scatter x1 -> x2, waiting for transfers between devices: 36.2 us -> 0.04 us  [the longest x1 0.02 us: per_device(): lax.psum_scatter(cache_mixed, 'tensor', scatter_dimension=0, tiled=True)]
    all_to_all x1 -> x0, blocking collectives: 23.2 us -> none  [per_device(): lax.all_to_all(column_block, 'tensor', split_axis=0, concat_axis=1, tiled...]
    pmax x0 -> x1, blocking collectives: none -> 15.5 us  [per_device(): cache_top = lax.pmax(cache_top, 'tensor')]
    unnamed x13 -> x18, local copies, waits for them, and re-layouts: 5.23 us -> 19.7 us
    dot_general x7 -> x8, matrix products: 46.5 us -> 36.4 us  [the longest x1 15.5 us: per_device(): jnp.dot(prompt_weighted, weight_heads[:, :, 1].reshape(features, kv_heads...]
    reduce_sum x6 -> x1, other arithmetic: 6.5 us -> 0.18 us  [per_device(): step_total = jnp.sum(step_weights, axis=-1)]
  transfers between devices with their start and end apart: 2 -> 3, of which waited for: 2 -> 1; matrix products, arithmetic and copies ran while one was open for 7% -> 17% of each run, Pallas kernels for 0% -> 0%
where the time goes in v1:
time: 233 us; the launch traced here: 232 us
  blocking collectives  113 us (48%)
  matrix products  43.7 us (19%)
  local copies, waits for them, and re-layouts  32.9 us (14%)
  other arithmetic  26.3 us (11%)
  between operations  13.5 us (6%)
  waiting for transfers between devices  2.5 us (1%)
    all_gather x1, blocking collectives, per_device(): query_rows = lax.all_gather(my_queries, shards, axis=1, tiled=True)  27.6 us
    all_gather x1, blocking collectives, per_device(): lax.all_gather(mixed.astype(jnp.bfloat16), shards, axis=2, tiled=True)  24.8 us
    all_gather x1, blocking collectives, per_device(): log_all = lax.all_gather(prompt_log, shards, axis=2, tiled=True)  21.4 us
    unnamed x18, local copies, waits for them, and re-layouts  19.7 us
    dot_general x1, matrix products, per_device(): jnp.dot(prompt_weighted, weight_heads[:, :, 1].reshape(features, kv_heads...  15.5 us
    pmax x1, blocking collectives, per_device(): cache_top = lax.pmax(cache_top, 'tensor')  15.5 us
    psum x1, blocking collectives, per_device(): lax.psum((prompt_square, decode_square, decode_terms, cache_total), 'tens...  14.8 us
    convert_element_type x1, other arithmetic, per_device(): prompt_weighted = (prompt_wide * gain_wide).astype(jnp.bfloat16)  13 us
  transfers between devices with their start and end apart: 3, of which 1 were waited for; matrix products, arithmetic and copies ran while one was open for 17% of the time, Pallas kernels for 0%

profile of v1, /device:TPU:0, one launch (start us, length us, event | category | flops | bytes accessed | tf_op | source)
XLA Modules:
  0.0 231.6 jit_solution(6128773920156378063)
XLA Ops:
  6.6 0.7 compare_and_fusion
  7.3 1.3 gather_fusion.1
  8.7 0.7 convert_element_type.64
  9.4 16.7 %copy.145 = bf16[3072,2048]{0,1:T(8,128)(2,1)} copy(bf16[3072,2048]{1,0:T(8,128)(2,1)} %param.11) | data formatting | bytes 25165824 | tf_op args[3]
  26.1 27.6 %all_gather.12 = bf16[2,32,3072]{2,0,1:T(2,128)(2,1)S(1)} all-gather(bf16[2,4,3072]{2,0,1:T(2,128)(2,1)S(1)} %copy.185), channel_id=1, replica_groups=mesh['group'=2,'seq'=4,'tensor'=4] {'group','seq'}, dimensions={1}, use_global_device_ids=true | all-gather | bytes 442368 | tf_op jit(solution)/shard_map/all_gather | solution.py:58
  53.7 0.6 gather_fusion
  54.4 8.5 %all_gather.13 = bf16[2,2,12288]{2,0,1:T(2,128)(2,1)S(1)} all-gather(bf16[2,2,3072]{2,0,1:T(2,128)(2,1)S(1)} %fusion.44), channel_id=1, replica_groups=mesh['group'=2,'seq'=4,'tensor'=4] {'tensor'}, dimensions={2}, use_global_device_ids=true | all-gather | bytes 122880 | tf_op jit(solution)/shard_map/all_gather | solution.py:60
  63.0 13.0 %fusion = (bf16[1536,3072]{1,0:T(8,128)(2,1)}, f32[1536]{0:T(1024)S(1)}) fusion(bf16[1536,3072]{1,0:T(8,128)(2,1)} %param.8, f32[3072]{0:T(1024)S(1)} %convert_element_type.64), kind=kLoop, calls=%fused_computation.6 | loop fusion | flops 23591424 | bytes 18892800 | tf_op jit(solution)/shard_map/convert_element_type | solution.py:68
  76.1 7.3 %fusion.2 = f32[2,4,2048]{2,1,0:T(4,128)} fusion(bf16[3072,2048]{1,0:T(8,128)(2,1)} %param.11, bf16[2,4,3072]{2,1,0:T(4,128)(2,1)S(1)} %copy-done.3, f32[3072]{0:T(1024)S(1)} %convert_element_type.64), kind=kOutput, calls=%fused_computation.8 | convolution fusion | flops 100737024 | bytes 12709888 | tf_op jit(solution)/shard_map/srk,kc->src/dot_general | solution.py:72
  83.3 1.4 multiply_cosine_fusion
  84.8 12.2 %fusion.4 = f32[2,768,8,128]{1,3,2,0:T(8,128)S(1)} fusion(bf16[2,768,3072,1]{2,1,3,0:T(8,128)(2,1)S(1)} %bitcast.134, bf16[3072,8,2,128]{0,3,2,1:T(8,128)(2,1)} %bitcast.131), kind=kOutput, calls=%fused_computation.11 | convolution fusion | flops 9663676416 | bytes 22020096 | tf_op jit(solution)/shard_map/dot_general | solution.py:112
  97.0 1.0 subtract_convert_fusion
  98.0 1.7 fusion.5
  99.8 0.2 reshape.181
  100.1 6.0 %slice.56 = bf16[3072,8,1,128]{0,3,2,1:T(8,128)(2,1)} slice(bf16[3072,8,2,128]{0,3,2,1:T(8,128)(2,1)} %bitcast.132), slice={[0:3072], [0:8], [1:2], [0:128]} | slice | bytes 12582912 | tf_op jit(solution)/shard_map/slice | solution.py:125
  106.0 0.2 compare_reduce_fusion.1
  106.2 15.5 %fusion.14 = bf16[192,8,8,128]{3,1,2,0:T(8,128)(2,1)} fusion(bf16[1536,3072]{1,0:T(8,128)(2,1)} %get-tuple-element.20, bf16[3072,1024]{0,1:T(8,128)(2,1)} %bitcast.135), kind=kOutput, calls=%fused_computation.27 | convolution fusion | flops 9665249280 | bytes 18874368 | tf_op jit(solution)/shard_map/dot_general | solution.py:123
  121.9 2.6 %fusion.11 = f32[4,8,2,12,256]{4,3,2,1,0:T(8,128)S(1)} fusion(bf16[4,8,256,256]{3,2,1,0:T(8,128)(2,1)} %param.12, bf16[2,4,8,12,128]{4,3,2,1,0:T(8,128)(2,1)S(1)} %reshape.181), kind=kOutput, calls=%fused_computation.24 | convolution fusion | flops 50331648 | bytes 3080192 | tf_op jit(solution)/shard_map/srgqd,rgpd->rgsqp/dot_general | solution.py:82
  124.5 0.6 fusion.32
  125.1 0.1 copy.182
  125.3 15.5 %pmax.7 = f32[4,8,2,12]{3,2,1,0:T(2,128)S(1)} all-reduce(f32[4,8,2,12]{3,2,1,0:T(2,128)S(1)} %copy.182), channel_id=1, replica_groups=mesh['group'=2,'seq'=4,'tensor'=4] {'tensor'}, use_global_device_ids=true, to_apply=%region_6.7 | all-reduce | flops 768 | bytes 6144 | tf_op jit(solution)/shard_map/pmax | solution.py:92
  140.9 1.4 fusion.28
  142.3 0.1 copy.183
  142.6 14.8 %all-reduce = (f32[2,4]{1,0:T(2,128)S(1)}, f32[1536]{0:T(1024)S(1)}, f32[96,2,4]{0,1,2:T(2,128)S(1)}) all-reduce(f32[2,4]{1,0:T(2,128)S(1)} %fusion.35, f32[1536]{0:T(1024)S(1)} %get-tuple-element.21, f32[96,2,4]{0,1,2:T(2,128)S(1)} %reshape.193), channel_id=1, replica_groups=mesh['group'=2,'seq'=4,'tensor'=4] {'tensor'}, use_global_device_ids=true, to_apply=%region_2.3 | all-reduce | flops 2312 | bytes 18496 | tf_op jit(solution)/shard_map/psum | solution.py:103
  157.5 2.7 %copy.189 = bf16[192,8,8,128]{3,2,1,0:T(8,128)(2,1)S(1)} copy(bf16[192,8,8,128]{3,1,2,0:T(8,128)(2,1)} %fusion.14) | data formatting | bytes 6291456
  160.2 0.2 bitcast_bitcast_fusion
  160.4 2.4 %all-reduce.4.cloned.1.call-done = (f32[2,4,2048]{2,1,0:T(4,128)}, f32[2,8,2,12,768]{4,3,2,1,0:T(8,128)}) async-done(((f32[2,4,2048]{2,1,0:T(4,128)}, f32[2,8,2,12,768]{4,3,2,1,0:T(8,128)}), (f32[2,4,2048]{2,1,0:T(4,128)}, f32[2,8,2,12,768]{4,3,2,1,0:T(8,128)})) %all-reduce.4.cloned.1.call-update) | async-done | bytes 1245200 | tf_op jit(solution)/shard_map/psum | solution.py:103
  162.8 1.6 multiply_reduce_fusion
  164.4 1.9 multiply_convert_fusion
  166.4 0.9 fusion.22
  167.3 0.2 copy.159
  167.5 0.7 copy.160
  168.3 2.2 fusion.16
  170.5 0.3 copy.154
  170.7 0.8 copy.155
  171.6 0.7 compare_reduce_fusion
  172.4 0.1 multiply_cosine_fusion.1
  173.0 0.8 fusion.55
  173.8 0.4 convolution_bitcast_fusion
  174.2 0.3 copy.134
  174.6 0.2 fusion.50
  175.0 21.4 %all_gather.14 = f32[24,2,16]{0,1,2:T(2,128)S(1)} all-gather(f32[24,2,2]{0,1,2:T(2,128)S(1)} %copy.150), channel_id=1, replica_groups=mesh['group'=2,'seq'=4,'tensor'=4] {'group','seq'}, dimensions={2}, use_global_device_ids=true | all-gather | bytes 3456 | tf_op jit(solution)/shard_map/all_gather | solution.py:152
  196.4 0.6 gather_fusion.2
  197.2 0.8 convert_element_type.75
  198.0 24.8 %all_gather.15 = bf16[24,2,16,128]{3,0,2,1:T(8,128)(2,1)S(1)} all-gather(bf16[24,2,2,128]{3,0,2,1:T(8,128)(2,1)S(1)} %convert_element_type.75), channel_id=1, replica_groups=mesh['group'=2,'seq'=4,'tensor'=4] {'group','seq'}, dimensions={2}, use_global_device_ids=true | all-gather | bytes 221184 | tf_op jit(solution)/shard_map/all_gather | solution.py:153
  222.7 0.6 gather_fusion.3
  223.3 1.1 fusion.42
  224.4 0.6 copy.164
  (66 shorter events, 2.1 us)
Async XLA Ops:
  6.5 156.3 %all-reduce.4.cloned.1.call-start = ((), (), s32[]{:S(2)}) async-start(), calls=%async_computation.4 | async-start | bytes 3276800 | tf_op jit(solution)/shard_map/psum | solution.py:103
  9.4 16.7 %copy-start.2 = (bf16[2,4,12288]{2,1,0:T(4,128)(2,1)S(1)}, bf16[2,4,12288]{2,1,0:T(4,128)(2,1)}, u32[]{:S(2)}) copy-start(bf16[2,4,12288]{2,1,0:T(4,128)(2,1)} %param.13) | copy-start | bytes 589828
  63.0 13.0 %copy-start.3 = (bf16[2,4,3072]{2,1,0:T(4,128)(2,1)S(1)}, bf16[2,4,3072]{2,1,0:T(4,128)(2,1)}, u32[]{:S(2)}) copy-start(bf16[2,4,3072]{2,1,0:T(4,128)(2,1)} %param.9) | copy-start | bytes 147460
  76.1 8.7 %copy-start.1 = (bf16[1536,3072]{1,0:T(8,128)(2,1)S(1)}, bf16[1536,3072]{1,0:T(8,128)(2,1)}, u32[]{:S(2)}) copy-start(bf16[1536,3072]{1,0:T(8,128)(2,1)} %get-tuple-element.20) | copy-start | bytes 28311556
  99.7 97.4 %reduce-scatter.5.cloned.1.call-start = ((), (), s32[]{:S(2)}) async-start(), calls=%async_computation.3 | async-start | bytes 245760 | tf_op jit(solution)/shard_map/reduce_scatter | solution.py:146
  100.0 6.0 %copy-start.5 = (s32[16]{0:T(128)S(1)}, s32[16]{0:T(128)}, u32[]{:S(2)}) copy-start(s32[16]{0:T(128)} %param.15) | copy-start | bytes 196
  106.2 15.5 %copy-start = (s32[32]{0:T(128)S(1)}, s32[32]{0:T(128)}, u32[]{:S(2)}) copy-start(s32[32]{0:T(128)} %param.14) | copy-start | bytes 388
  168.2 4.4 %copy-start.4 = (f32[2,4,2048]{2,1,0:T(4,128)S(1)}, f32[2,4,2048]{2,1,0:T(4,128)}, u32[]{:S(2)}) copy-start(f32[2,4,2048]{2,1,0:T(4,128)} %get-tuple-element.10) | copy-start | bytes 196612
  168.2 55.1 %reduce-scatter.3.cloned.1.call-start = ((), (), s32[]{:S(2)}) async-start(), calls=%async_computation.2 | async-start | bytes 491520 | tf_op jit(solution)/shard_map/reduce_scatter | solution.py:101
Sparse Core Ops, SparseCore 0:
  99.9 62.9 all-reduce.3
  168.3 23.9 reduce-scatter.4
  195.1 24.3 reduce-scatter.2

commit v2 on v1

v2 whole, which is shorter than its diff:
```python
import functools
import math

import jax
import jax.numpy as jnp
from jax import lax
from jax.experimental import pallas as pl
from jax.experimental.pallas import tpu as pltpu
from jax.sharding import PartitionSpec as P

D = 12288
PLEN = 768
BLOCK = 256
LANES = 128


epsilon = 1e-05
rope_base = 1000000.0
very_negative = -1e30
f32 = jnp.float32
bf16 = jnp.bfloat16
contract_last = (((1,), (1,)), ((), ()))
contract_inner = (((1,), (0,)), ((), ()))


def angle_tables(positions, head_size):
    halfway = head_size // 2
    exponents = jnp.arange(halfway, dtype=f32) * (-2.0 / head_size)
    frequency = jnp.power(rope_base, exponents)
    angles = positions.astype(f32)[..., None] * frequency
    cosine, sine_part = jnp.cos(angles), jnp.sin(angles)
    return (
        jnp.concatenate([cosine, cosine], -1),
        jnp.concatenate([-sine_part, sine_part], -1),
    )


def rotated(values, cosine, sine_part):
    return values * cosine + pltpu.roll(values, values.shape[-1] // 2, 1) * sine_part


def kernel(
    sizes,
    prompt_ref,
    step_hidden_ref,
    gain_ref,
    weight_ref,
    cache_ref,
    query_ref,
    cos_ref,
    sin_ref,
    step_cos_ref,
    step_sin_ref,
    owner_ref,
    length_ref,
    new_ref,
    pick_ref,
    out_ref,
    xw,
    wk,
    wv,
    cbuf,
    acc,
    kbuf,
    vbuf,
    q1,
    q2,
    sq,
    sqd,
    s_send,
    s_recv,
    w_all,
    lse_all,
    linv,
    o_send,
    o_recv,
    o_all,
    c_send,
    c_recv,
    cl_send,
    cl_recv,
    d_send,
    d_recv,
    x_sem,
    w_sem,
    c_sem,
    shard_sems,
    tensor_sems,
):
    n_t, n_s, n_seq, kpc, unit, group, steps, rows = sizes
    tokens, features = prompt_ref.shape
    prompts = tokens // PLEN
    cache_rows = cbuf.shape[2]
    me = lax.axis_index("tensor")
    my_seq = lax.axis_index("seq")
    shard = lax.axis_index("group") * n_seq + my_seq
    scale = 1.0 / math.sqrt(LANES)
    unit_rows = unit * steps

    def chunk(k):
        return lax.rem(me + 1 + k, n_t)

    def head_of(t, j):
        return (t * kpc * unit + j * unit) // group

    def to_tensor(src, dst, which, k):
        return pltpu.make_async_remote_copy(
            src_ref=src,
            dst_ref=dst,
            send_sem=tensor_sems.at[which, 0, k],
            recv_sem=tensor_sems.at[which, 1, k],
            device_id={"tensor": chunk(k)},
            device_id_type=pl.DeviceIdType.MESH,
        )

    def to_shard(src, dst, which, k):
        peer = lax.rem(shard + 1 + k, n_s)
        return pltpu.make_async_remote_copy(
            src_ref=src,
            dst_ref=dst,
            send_sem=shard_sems.at[which, 0, k],
            recv_sem=shard_sems.at[which, 1, k],
            device_id={"group": peer // n_seq, "seq": lax.rem(peer, n_seq)},
            device_id_type=pl.DeviceIdType.MESH,
        )

    def each(count, body):
        def step(k, carry):
            body(k)
            return carry

        lax.fori_loop(0, count, step, 0)

    def gather(maker, ref, mine, which, count):
        each(count, lambda k: maker(ref.at[mine], ref.at[mine], which, k).start())

    def gathered(maker, ref, mine, which, count, total):
        def body(k):
            source = lax.rem(mine - 1 - k + total, total)
            maker(ref.at[mine], ref.at[source], which, k).wait_recv()

        each(count, body)

    def sent(maker, ref, mine, which, count):
        each(count, lambda k: maker(ref.at[mine], ref.at[mine], which, k).wait_send())

    blocks = tokens // BLOCK

    def x_copy(b):
        at = pl.ds(pl.multiple_of(b * BLOCK, BLOCK), BLOCK)
        return pltpu.make_async_copy(prompt_ref.at[at], xw.at[at], x_sem.at[b])

    def w_copy(k, j, value):
        column = pl.multiple_of(head_of(chunk(k), j) * 2 * LANES + value * LANES, LANES)
        dst = (wv if value else wk).at[k, :, pl.ds(j * LANES, LANES)]
        return pltpu.make_async_copy(
            weight_ref.at[:, pl.ds(column, LANES)], dst, w_sem.at[value, j, k]
        )

    c_copy = pltpu.make_async_copy(cache_ref, cbuf, c_sem)
    each(blocks, lambda b: x_copy(b).start())
    for value in range(2):
        for j in range(kpc):
            each(n_t, lambda k: w_copy(k, j, value).start())
    c_copy.start()

    barrier = pltpu.get_barrier_semaphore()

    def greet_tensor(k):
        pl.semaphore_signal(
            barrier, inc=1, device_id={"tensor": chunk(k)}, device_id_type=pl.DeviceIdType.MESH
        )

    def greet_shard(k):
        peer = lax.rem(shard + 1 + k, n_s)
        pl.semaphore_signal(
            barrier,
            inc=1,
            device_id={"group": peer // n_seq, "seq": lax.rem(peer, n_seq)},
            device_id_type=pl.DeviceIdType.MESH,
        )

    each(n_t - 1, greet_tensor)
    each(n_s - 1, greet_shard)
    pl.semaphore_wait(barrier, n_t + n_s - 2)

    q1[shard] = query_ref[me]
    gather(to_shard, q1, shard, 0, n_s - 1)

    def weigh(b):
        x_copy(b).wait()
        at = pl.ds(pl.multiple_of(b * BLOCK, BLOCK), BLOCK)
        square = jnp.zeros((BLOCK, LANES), f32)
        for c in range(features // LANES):
            lanes = pl.ds(c * LANES, LANES)
            wide = xw[at, lanes].astype(f32)
            square += wide * wide
            xw[at, lanes] = (wide * gain_ref[:, lanes].astype(f32)).astype(bf16)
        total = jnp.sum(square.T, axis=0, keepdims=True)
        sq[me, b] = jnp.broadcast_to(total, (8, BLOCK))

    each(blocks, weigh)
    wide = step_hidden_ref[...].astype(f32)
    sqd[me] = jnp.broadcast_to(
        jnp.sum(wide * wide, axis=1, keepdims=True), (wide.shape[0], LANES)
    )
    pad = wide.shape[0]
    xw[pl.ds(tokens, pad), :] = (wide * gain_ref[...].astype(f32)).astype(bf16)
    gather(to_tensor, sq, me, 0, n_t - 1)
    gather(to_tensor, sqd, me, 1, n_t - 1)

    def keys(k):
        for j in range(kpc):
            w_copy(k, j, 0).wait()
        acc[...] = jnp.dot(xw[...], wk[k], preferred_element_type=f32)
        for j in range(kpc):
            lanes = pl.ds(j * LANES, LANES)
            for p in range(prompts):
                part = acc[pl.ds(p * PLEN, PLEN), lanes]
                kbuf[k, p, j] = rotated(part, cos_ref[p], sin_ref[p]).astype(bf16)
            d_send[k, 0, j] = acc[pl.ds(tokens, pad), lanes]

    each(n_t, keys)

    gathered(to_shard, q1, shard, 0, n_s - 1, n_s)
    for p in range(prompts):
        owner = owner_ref[p]
        q2[me, p] = q1[owner // rows, lax.rem(owner, rows)]
    gather(to_tensor, q2, me, 2, n_t - 1)
    gathered(to_tensor, q2, me, 2, n_t - 1, n_t)

    def score(k):
        t = chunk(k)
        for p in range(prompts):
            for j in range(kpc):
                s_send[k, p, j] = lax.dot_general(
                    q2[t, p, j], kbuf[k, p, j], contract_last, preferred_element_type=f32
                )

        @pl.when(k < n_t - 1)
        def _():
            to_tensor(s_send.at[k], s_recv.at[k], 3, k).start()

    each(n_t, score)

    def values(k):
        for j in range(kpc):
            w_copy(k, j, 1).wait()
        acc[...] = jnp.dot(xw[...], wv[k], preferred_element_type=f32)
        for j in range(kpc):
            lanes = pl.ds(j * LANES, LANES)
            for p in range(prompts):
                vbuf[k, p, j] = acc[pl.ds(p * PLEN, PLEN), lanes].astype(bf16)
            d_send[k, 1, j] = acc[pl.ds(tokens, pad), lanes]

        @pl.when(k < n_t - 1)
        def _():
            to_tensor(d_send.at[k], d_recv.at[k], 4, k).start()

    each(n_t, values)

    c_copy.wait()
    position = me * cache_rows + lax.broadcasted_iota(jnp.int32, (unit_rows, cache_rows), 1)
    lane = lax.broadcasted_iota(jnp.int32, (unit_rows, LANES), 1)
    per_row = LANES // rows

    def resident(k):
        t = chunk(k)
        for j in range(kpc):
            g = head_of(t, j)
            packed = jnp.zeros((unit_rows, LANES), f32)
            for r in range(rows):
                found = lax.dot_general(
                    query_ref[t, r, j],
                    cbuf[r, g, :, pl.ds(0, LANES)],
                    contract_last,
                    preferred_element_type=f32,
                )
                mask = position < length_ref[r]
                found = jnp.where(mask, found * scale, very_negative)
                top = jnp.max(found, axis=1, keepdims=True)
                weights = jnp.where(mask, jnp.exp(found - top), 0.0)
                total = jnp.sum(weights, axis=1, keepdims=True)
                some = total > 0.0
                total = jnp.where(some, total, 1.0)
                mixed = lax.dot_general(
                    weights.astype(bf16),
                    cbuf[r, g, :, pl.ds(LANES, LANES)],
                    contract_inner,
                    preferred_element_type=f32,
                )
                c_send[k, r, j] = (mixed / total).astype(bf16)
                log = jnp.where(some, top + jnp.log(total), very_negative)
                packed = jnp.where(lane // per_row == r, log, packed)
            cl_send[k, j] = packed

        @pl.when(k < n_t - 1)
        def _():
            to_tensor(c_send.at[k], c_recv.at[k], 5, k).start()
            to_tensor(cl_send.at[k], cl_recv.at[k], 6, k).start()

    each(n_t, resident)

    gathered(to_tensor, sq, me, 0, n_t - 1, n_t)
    gathered(to_tensor, sqd, me, 1, n_t - 1, n_t)
    each(n_t - 1, lambda k: to_tensor(s_send.at[k], s_recv.at[k], 3, k).wait_recv())
    per_prompt = PLEN // BLOCK
    for p in range(prompts):
        parts = []
        for b in range(per_prompt):
            total = sq[0, p * per_prompt + b]
            for t in range(1, n_t):
                total += sq[t, p * per_prompt + b]
            parts.append(lax.rsqrt(total[0:1] / D + epsilon))
        factor = jnp.concatenate(parts, axis=1)
        for j in range(kpc):
            total = s_send[n_t - 1, p, j]
            for k in range(n_t - 1):
                total += s_recv[k, p, j]
            total = total * (factor * scale)
            top = jnp.max(total, axis=1, keepdims=True)
            weights = jnp.exp(total - top)
            whole = jnp.sum(weights, axis=1, keepdims=True)
            w_all[me, p, j] = (weights * factor).astype(bf16)
            lse_all[shard, p, j] = jnp.broadcast_to(top + jnp.log(whole), (unit_rows, LANES))
            linv[p, j] = jnp.broadcast_to(1.0 / whole, (unit_rows, LANES))
    gather(to_tensor, w_all, me, 7, n_t - 1)
    gather(to_shard, lse_all, shard, 1, n_s - 1)

    def mix(k):
        t = chunk(k)

        @pl.when(k < n_t - 1)
        def _():
            to_tensor(w_all.at[me], w_all.at[t], 7, n_t - 2 - k).wait_recv()

        for p in range(prompts):
            for j in range(kpc):
                o_send[k, p, j] = lax.dot_general(
                    w_all[t, p, j], vbuf[k, p, j], contract_inner, preferred_element_type=f32
                )

        @pl.when(k < n_t - 1)
        def _():
            to_tensor(o_send.at[k], o_recv.at[k], 8, k).start()

    each(n_t, mix)
    each(n_t - 1, lambda k: to_tensor(o_send.at[k], o_recv.at[k], 8, k).wait_recv())
    for p in range(prompts):
        for j in range(kpc):
            total = o_send[n_t - 1, p, j]
            for k in range(n_t - 1):
                total += o_recv[k, p, j]
            o_all[shard, p, j] = (total * linv[p, j]).astype(bf16)
    gather(to_shard, o_all, shard, 2, n_s - 1)

    each(n_t - 1, lambda k: to_tensor(d_send.at[k], d_recv.at[k], 4, k).wait_recv())
    each(n_t - 1, lambda k: to_tensor(c_send.at[k], c_recv.at[k], 5, k).wait_recv())
    each(n_t - 1, lambda k: to_tensor(cl_send.at[k], cl_recv.at[k], 6, k).wait_recv())
    total = sqd[0]
    for t in range(1, n_t):
        total += sqd[t]
    factor = lax.rsqrt(total / D + epsilon)
    own_row = lax.broadcasted_iota(jnp.int32, (unit_rows, pad), 0)
    column = lax.broadcasted_iota(jnp.int32, (unit_rows, pad), 1)
    causal = (column // rows <= own_row // unit) & (column < steps * rows)
    states = {}
    for j in range(kpc):
        terms = []
        for value in range(2):
            total = d_send[n_t - 1, value, j]
            for k in range(n_t - 1):
                total += d_recv[k, value, j]
            terms.append(total * factor)
        key = rotated(terms[0], step_cos_ref[...], step_sin_ref[...]).astype(bf16)
        value = terms[1].astype(bf16)
        for r in range(rows):
            found = lax.dot_general(
                query_ref[me, r, j], key, contract_last, preferred_element_type=f32
            )
            mask = causal & (lax.rem(column, rows) == r)
            found = jnp.where(mask, found * scale, very_negative)
            top = jnp.max(found, axis=1, keepdims=True)
            logs = [cl_send[n_t - 1, j][:, r * per_row : r * per_row + 1]]
            outs = [c_send[n_t - 1, r, j]]
            for k in range(n_t - 1):
                logs.append(cl_recv[k, j][:, r * per_row : r * per_row + 1])
                outs.append(c_recv[k, r, j])
            for log in logs:
                top = jnp.maximum(top, log)
            weights = jnp.where(mask, jnp.exp(found - top), 0.0)
            whole = jnp.sum(weights, axis=1, keepdims=True)
            mixed = lax.dot_general(
                weights.astype(bf16), value, contract_inner, preferred_element_type=f32
            )
            for log, out in zip(logs, outs):
                share = jnp.exp(log - top)
                whole += share
                mixed += share * out.astype(f32)
            states[j, r] = (top, whole, mixed)

    gathered(to_shard, lse_all, shard, 1, n_s - 1, n_s)
    gathered(to_shard, o_all, shard, 2, n_s - 1, n_s)
    for j in range(kpc):
        for r in range(rows):
            top, whole, mixed = states[j, r]
            pick = pick_ref[r]
            source, p = pick // prompts, lax.rem(pick, prompts)
            log = lse_all[source, p, j]
            log = jnp.where(new_ref[r] > 0, log, very_negative)
            out = o_all[source, p, j].astype(f32)
            last = jnp.maximum(top, log)
            left, right = jnp.exp(top - last), jnp.exp(log - last)
            out_ref[r, j] = ((mixed * left + out * right) / (whole * left + right)).astype(bf16)

    sent(to_shard, q1, shard, 0, n_s - 1)
    sent(to_shard, lse_all, shard, 1, n_s - 1)
    sent(to_shard, o_all, shard, 2, n_s - 1)
    sent(to_tensor, sq, me, 0, n_t - 1)
    sent(to_tensor, sqd, me, 1, n_t - 1)
    sent(to_tensor, q2, me, 2, n_t - 1)
    sent(to_tensor, w_all, me, 7, n_t - 1)
    for which, src, dst in (
        (3, s_send, s_recv),
        (4, d_send, d_recv),
        (5, c_send, c_recv),
        (6, cl_send, cl_recv),
        (8, o_send, o_recv),
    ):
        each(n_t - 1, lambda k: to_tensor(src.at[k], dst.at[k], which, k).wait_send())


def per_device(
    prompt_hidden, decode_hidden, norm_gain, kv_weight, kv_cache, queries, lengths, prompt_row
):
    shards = ("group", "seq")
    n_t = lax.axis_size("tensor")
    n_s = lax.axis_size(shards)
    n_seq = lax.axis_size("seq")
    shard_rank = lax.axis_index(shards)
    tokens, features = prompt_hidden.shape
    steps, rows, query_width = queries.shape
    kv_heads, cache_rows = kv_cache.shape[1:3]
    head_size = kv_cache.shape[3] // 2
    query_heads = query_width // head_size
    group = query_heads // kv_heads
    local_heads = query_heads // n_t
    unit = min(local_heads, group)
    kpc = local_heads // unit
    prompts = tokens // PLEN
    unit_rows = unit * steps
    pad = -(-steps * rows // 16) * 16
    cols = kpc * head_size

    my_owners = lax.dynamic_slice_in_dim(prompt_row, shard_rank * prompts, prompts, 0)
    my_rows = shard_rank * rows + jnp.arange(rows, dtype=jnp.int32)
    my_lengths = lax.dynamic_slice_in_dim(lengths, shard_rank * rows, rows, 0)
    owned = prompt_row[None, :] == my_rows[:, None]
    is_new = jnp.any(owned, axis=1).astype(jnp.int32)
    pick = jnp.sum(
        jnp.where(owned, jnp.arange(prompt_row.shape[0], dtype=jnp.int32)[None, :], 0), axis=1
    )
    positions = (
        jnp.take(lengths, my_owners)[:, None] + jnp.arange(PLEN, dtype=jnp.int32)[None, :]
    )
    cosine, sine_part = angle_tables(positions, head_size)
    step_ids = jnp.arange(steps, dtype=jnp.int32)
    step_pos = (my_lengths + PLEN * is_new)[None, :] + step_ids[:, None]
    step_pos = jnp.pad(step_pos.reshape(-1), (0, pad - steps * rows))
    step_cos, step_sin = angle_tables(step_pos, head_size)
    step_hidden = jnp.pad(
        decode_hidden.reshape(steps * rows, features), ((0, pad - steps * rows), (0, 0))
    )
    query_units = jnp.transpose(
        queries.reshape(steps, rows, n_t, kpc, unit, head_size), (2, 1, 3, 0, 4, 5)
    ).reshape(n_t, rows, kpc, unit_rows, head_size)

    vmem = pl.BlockSpec(memory_space=pltpu.VMEM)
    smem = pl.BlockSpec(memory_space=pltpu.SMEM)
    hbm = pl.BlockSpec(memory_space=pl.ANY)
    per_unit = (kpc, unit_rows)
    dma = pltpu.SemaphoreType.DMA
    flops = 2 * tokens * features * 2 * cols * n_t
    result = pl.pallas_call(
        functools.partial(kernel, (n_t, n_s, n_seq, kpc, unit, group, steps, rows)),
        out_shape=jax.ShapeDtypeStruct((rows,) + per_unit + (head_size,), bf16),
        in_specs=[hbm, vmem, vmem, hbm, hbm, vmem, vmem, vmem, vmem, vmem]
        + [smem, smem, smem, smem],
        out_specs=vmem,
        scratch_shapes=[
            pltpu.VMEM((tokens + pad, features), bf16),
            pltpu.VMEM((n_t, features, cols), bf16),
            pltpu.VMEM((n_t, features, cols), bf16),
            pltpu.VMEM(kv_cache.shape, bf16),
            pltpu.VMEM((tokens + pad, cols), f32),
            pltpu.VMEM((n_t, prompts, kpc, PLEN, head_size), bf16),
            pltpu.VMEM((n_t, prompts, kpc, PLEN, head_size), bf16),
            pltpu.VMEM((n_s, rows) + per_unit + (head_size,), bf16),
            pltpu.VMEM((n_t, prompts) + per_unit + (head_size,), bf16),
            pltpu.VMEM((n_t, tokens // BLOCK, 8, BLOCK), f32),
            pltpu.VMEM((n_t, pad, LANES), f32),
            pltpu.VMEM((n_t, prompts) + per_unit + (PLEN,), f32),
            pltpu.VMEM((n_t - 1, prompts) + per_unit + (PLEN,), f32),
            pltpu.VMEM((n_t, prompts) + per_unit + (PLEN,), bf16),
            pltpu.VMEM((n_s, prompts) + per_unit + (LANES,), f32),
            pltpu.VMEM((prompts,) + per_unit + (LANES,), f32),
            pltpu.VMEM((n_t, prompts) + per_unit + (head_size,), f32),
            pltpu.VMEM((n_t - 1, prompts) + per_unit + (head_size,), f32),
            pltpu.VMEM((n_s, prompts) + per_unit + (head_size,), bf16),
            pltpu.VMEM((n_t, rows) + per_unit + (head_size,), bf16),
            pltpu.VMEM((n_t - 1, rows) + per_unit + (head_size,), bf16),
            pltpu.VMEM((n_t,) + per_unit + (LANES,), f32),
            pltpu.VMEM((n_t - 1,) + per_unit + (LANES,), f32),
            pltpu.VMEM((n_t, 2, kpc, pad, head_size), f32),
            pltpu.VMEM((n_t - 1, 2, kpc, pad, head_size), f32),
            dma((tokens // BLOCK,)),
            dma((2, kpc, n_t)),
            dma,
            dma((3, 2, n_s - 1)),
            dma((9, 2, n_t - 1)),
        ],
        compiler_params=pltpu.CompilerParams(
            collective_id=0, has_side_effects=True, vmem_limit_bytes=60 * 1024 * 1024
        ),
        cost_estimate=pl.CostEstimate(
            flops=flops, bytes_accessed=30_000_000, transcendentals=1_000_000
        ),
    )(
        prompt_hidden,
        step_hidden,
        norm_gain.reshape(1, features),
        kv_weight,
        kv_cache,
        query_units,
        cosine,
        sine_part,
        step_cos,
        step_sin,
        my_owners,
        my_lengths,
        is_new,
        pick,
    )
    result = result.reshape(rows, kpc, steps, unit, head_size)
    return jnp.transpose(result, (2, 0, 1, 3, 4)).reshape(steps, rows, local_heads * head_size)


def solution(mesh):
    return jax.shard_map(
        per_device,
        mesh=mesh,
        in_specs=(
            P(("group", "seq"), "tensor"),
            P(None, ("group", "seq"), "tensor"),
            P("tensor"),
            P("tensor", None),
            P(("group", "seq"), None, "tensor", None),
            P(None, ("group", "seq"), None),
            P(),
            P(),
        ),
        out_specs=P(None, ("group", "seq"), "tensor"),
        check_vma=False,
    )
```

time: 233 us -> 83.7 us (0.36)
  blocking collectives: 113 us -> 0 us
  Pallas kernels: 0 us -> 65.4 us
  matrix products: 43.7 us -> 0 us
  local copies, waits for them, and re-layouts: 32.9 us -> 7.66 us
  other arithmetic: 26.3 us -> 10.2 us
  between operations: 13.5 us -> 0.06 us
  waiting for transfers between devices: 2.5 us -> 0 us
    all_gather x4 -> x0, blocking collectives: 82.3 us -> none  [the longest x1 27.6 us: per_device(): query_rows = lax.all_gather(my_queries, shards, axis=1, tiled=True)]
    pallas_call x0 -> x1, Pallas kernels: none -> 65.4 us  [per_device(): pl.pallas_call(functools.partial(kernel, (n_t, n_s, n_seq, kpc, unit, gro...]
    dot_general x9 -> x0, matrix products: 43.7 us -> none  [the longest x1 15.5 us: per_device(): jnp.dot(prompt_weighted, weight_heads[:, :, 1].reshape(features, kv_heads...]
    unnamed x18 -> x2, local copies, waits for them, and re-layouts: 19.7 us -> 0.01 us
    convert_element_type x8 -> x3, other arithmetic: 19.1 us -> 0.66 us  [the longest x1 0.58 us: per_device(): is_new = jnp.any(owned, axis=1).astype(jnp.int32)]
    pmax x1 -> x0, blocking collectives: 15.5 us -> none  [per_device(): cache_top = lax.pmax(cache_top, 'tensor')]
    psum x1 -> x0, blocking collectives: 14.8 us -> none  [per_device(): lax.psum((prompt_square, decode_square, decode_terms, cache_total), 'tens...]
    slice x3 -> x0, local copies, waits for them, and re-layouts: 6.01 us -> none  [the longest x1 5.95 us: per_device(): weight_heads[:, :, 1].reshape(features, kv_heads * head_size)]
  transfers between devices with their start and end apart: 3 -> 0, of which waited for: 1 -> 0; matrix products, arithmetic and copies ran while one was open for 17% -> 0% of each run, Pallas kernels for 0% -> 0%
where the time goes in v2:
time: 83.7 us; the launch traced here: 83.3 us
  Pallas kernels  65.4 us (78%)
  other arithmetic  10.2 us (12%)
  local copies, waits for them, and re-layouts  7.66 us (9%)
    pallas_call x1, Pallas kernels, per_device(): pl.pallas_call(functools.partial(kernel, (n_t, n_s, n_seq, kpc, unit, gro...  65.4 us
    neg x2, other arithmetic, angle_tables(): -sine_part  2.94 us
    concatenate x2, other arithmetic, angle_tables(): jnp.concatenate([cosine, cosine], -1)  2.32 us

profile of v2, /device:TPU:0, one launch (start us, length us, event | category | flops | bytes accessed | tf_op | source)
XLA Modules:
  0.0 83.3 jit_solution(8118643340490798485)
XLA Ops:
  0.0 0.7 compare_select_fusion
  0.7 0.0 copy-start
  0.7 1.3 %gather_fusion = s32[2]{0:T(128)S(1)} fusion(s32[32]{0:T(128)} %param.14, s32[1024]{0:T(1024)S(1)} %pad_clamp_fusion), kind=kCustom, calls=%fused_computation | custom fusion | bytes 24 | tf_op jit(solution)/shard_map/jit(_take)/gather | solution.py:464
  2.0 0.1 add_convert_fusion
  2.1 2.8 %fusion = (f32[2,768,64]{2,1,0:T(8,128)S(1)}, f32[2,768,64]{2,1,0:T(8,128)S(1)}, f32[2,768,64]{2,1,0:T(8,128)S(1)}) fusion(f32[64]{0:T(128)S(1)} %multiply_power_fusion, f32[2,768]{1,0:T(2,128)S(1)} %add_convert_fusion), kind=kLoop, calls=%fused_computation.5 | loop fusion | flops 196608 | bytes 1186048 | tf_op jit(solution)/shard_map/neg | solution.py:34
  5.0 1.6 %pad_maximum_fusion = (f32[2,768,128]{2,1,0:T(8,128)}, f32[2,768,128]{2,1,0:T(8,128)}) fusion(f32[2,768,64]{2,1,0:T(8,128)S(1)} %get-tuple-element.11, f32[2,768,64]{2,1,0:T(8,128)S(1)} %get-tuple-element.10, f32[2,768,64]{2,1,0:T(8,128)S(1)} %get-tuple-element.9), kind=kLoop, calls=%fused_computation.3 | loop fusion | flops 393216 | bytes 2752512 | tf_op jit(solution)/shard_map/concatenate | solution.py:33
  6.6 0.8 %compare_reduce_fusion = pred[4]{0:T(512)(128)(4,1)S(1)} fusion(s32[16]{0:T(128)} %param.15, s32[4]{0:T(128)S(1)} %iota_add_fusion.1), kind=kLoop, calls=%fused_computation.15 | loop fusion | flops 124 | bytes 84 | tf_op jit(solution)/shard_map/reduce_or | solution.py:459
  7.4 1.3 %select_add_fusion = (s32[4]{0:T(128)S(1)}, s32[4]{0:T(128)}) fusion(pred[4]{0:T(512)(128)(4,1)S(1)} %compare_reduce_fusion, s32[32]{0:T(128)} %param.14, s32[]{:T(128)S(6)} %select_n.24), kind=kLoop, calls=%fused_computation.20 | loop fusion | flops 8 | bytes 56 | tf_op jit(solution)/shard_map/add | solution.py:468
  8.7 0.1 add.77
  8.8 0.1 fusion.1
  9.0 0.7 pad_maximum_fusion.2
  9.6 0.6 convert_element_type.17.new_ref
  10.2 1.4 %fusion.2.pick_ref = s32[4]{0:T(128)} fusion(s32[16]{0:T(128)} %param.15, s32[4]{0:T(128)S(1)} %iota_add_fusion.1), kind=kLoop, calls=%fused_computation.16 | loop fusion | flops 188 | bytes 96 | tf_op jit(solution)/shard_map/reduce_sum | solution.py:460
  11.6 1.2 %reshape.70 = bf16[2,4,4,2,12,128]{5,4,3,2,1,0:T(8,128)(2,1)S(1)} reshape(bf16[2,4,12288]{2,1,0:T(4,128)(2,1)} %param.13) | data formatting | bytes 393216 | tf_op jit(solution)/shard_map/reshape | solution.py:475
  12.8 0.2 copy.15
  13.0 0.7 copy.16.query_ref
  13.7 0.8 reshape.68
  14.5 0.7 pad.8.step_hidden_ref
  15.1 1.3 %reshape.69.gain_ref = bf16[1,3072]{1,0:T(2,128)(2,1)} reshape(bf16[3072]{0:T(1024)(128)(2,1)} %param.10) | data formatting | bytes 12288 | tf_op jit(solution)/shard_map/reshape | solution.py:531
  16.4 0.0 copy-done
  16.4 65.4 %shard_map.82 = bf16[4,2,24,128]{3,2,1,0:T(8,128)(2,1)} custom-call(bf16[1536,3072]{1,0:T(8,128)(2,1)} %prompt_ref.1, bf16[16,3072]{1,0:T(8,128)(2,1)} %pad.8.step_hidden_ref, bf16[1,3072]{1,0:T(2,128)(2,1)} %reshape.69.gain_ref, bf16[3072,2048]{1,0:T(8,128)(2,1)} %weight_ref.1, bf16[4,8,256,256]{3,2,1,0:T(8,128)(2,1)} %cache_ref.1, ...), custom_call_target="tpu_custom_call" | custom-call | flops 19327352832 | bytes 30000000 | tf_op jit(solution)/shard_map/pallas_call | solution.py:484
  81.8 0.8 %copy.17 = bf16[4,2,24,128]{3,1,2,0:T(2,128)(2,1)S(1)} copy(bf16[4,2,24,128]{3,2,1,0:T(8,128)(2,1)} %shard_map.82) | data formatting | bytes 98304 | tf_op jit(solution)/shard_map/pallas_call | solution.py:484
  82.6 0.6 reshape.73
  (7 shorter events, 0.0 us)
Async XLA Ops:
  0.7 15.7 %copy-start = (s32[2]{0:T(128)}, s32[2]{0:T(128)S(1)}, u32[]{:S(2)}) copy-start(s32[2]{0:T(128)S(1)} %get-tuple-element.8.owner_ref) | copy-start | bytes 28

commit v3 on v2

--- a/solution.py
+++ b/solution.py
@@ -3,6 +3,7 @@
 
 import jax
 import jax.numpy as jnp
+import numpy as np
 from jax import lax
 from jax.experimental import pallas as pl
 from jax.experimental.pallas import tpu as pltpu
@@ -23,16 +24,14 @@
 contract_inner = (((1,), (0,)), ((), ()))
 
 
-def angle_tables(positions, head_size):
+def angle_tables(head_size):
     halfway = head_size // 2
-    exponents = jnp.arange(halfway, dtype=f32) * (-2.0 / head_size)
-    frequency = jnp.power(rope_base, exponents)
-    angles = positions.astype(f32)[..., None] * frequency
-    cosine, sine_part = jnp.cos(angles), jnp.sin(angles)
-    return (
-        jnp.concatenate([cosine, cosine], -1),
-        jnp.concatenate([-sine_part, sine_part], -1),
-    )
+    frequency = rope_base ** (np.arange(halfway) * (-2.0 / head_size))
+    frequency = np.concatenate([frequency, frequency])[None, :]
+    angles = np.arange(PLEN)[:, None] * frequency
+    signs = np.where(np.arange(head_size) < halfway, -1.0, 1.0)[None, :]
+    tables = np.cos(angles), np.sin(angles) * signs, np.concatenate([frequency, signs])
+    return [jnp.asarray(table, f32) for table in tables]
 
 
 def rotated(values, cosine, sine_part):
@@ -49,12 +48,9 @@
     query_ref,
     cos_ref,
     sin_ref,
-    step_cos_ref,
-    step_sin_ref,
-    owner_ref,
+    line_ref,
     length_ref,
-    new_ref,
-    pick_ref,
+    prompt_row_ref,
     out_ref,
     xw,
     wk,
@@ -81,6 +77,9 @@
     cl_recv,
     d_send,
     d_recv,
+    cos_at,
+    sin_at,
+    out_wide,
     x_sem,
     w_sem,
     c_sem,
@@ -90,6 +89,7 @@
     n_t, n_s, n_seq, kpc, unit, group, steps, rows = sizes
     tokens, features = prompt_ref.shape
     prompts = tokens // PLEN
+    pad = d_send.shape[3]
     cache_rows = cbuf.shape[2]
     me = lax.axis_index("tensor")
     my_seq = lax.axis_index("seq")
@@ -183,6 +183,17 @@
     each(n_t - 1, greet_tensor)
     each(n_s - 1, greet_shard)
     pl.semaphore_wait(barrier, n_t + n_s - 2)
+
+    owners = [prompt_row_ref[shard * prompts + p] for p in range(prompts)]
+    row_lengths = [length_ref[shard * rows + r] for r in range(rows)]
+    row_new = [jnp.int32(0) for r in range(rows)]
+    row_pick = [jnp.int32(0) for r in range(rows)]
+    for i in range(prompt_row_ref.shape[0]):
+        row = prompt_row_ref[i]
+        for r in range(rows):
+            mine = row == shard * rows + r
+            row_new[r] = jnp.where(mine, 1, row_new[r])
+            row_pick[r] = jnp.where(mine, i, row_pick[r])
 
     q1[shard] = query_ref[me]
     gather(to_shard, q1, shard, 0, n_s - 1)
@@ -200,12 +211,19 @@
         sq[me, b] = jnp.broadcast_to(total, (8, BLOCK))
 
     each(blocks, weigh)
-    wide = step_hidden_ref[...].astype(f32)
+    wide = [step_hidden_ref[step].astype(f32) for step in range(steps)]
+    wide.append(jnp.zeros((pad - steps * rows, features), f32))
+    wide = jnp.concatenate(wide, axis=0)
     sqd[me] = jnp.broadcast_to(
-        jnp.sum(wide * wide, axis=1, keepdims=True), (wide.shape[0], LANES)
+        jnp.sum(wide * wide, axis=1, keepdims=True), (pad, LANES)
     )
-    pad = wide.shape[0]
     xw[pl.ds(tokens, pad), :] = (wide * gain_ref[...].astype(f32)).astype(bf16)
+    for p in range(prompts):
+        start = length_ref[owners[p]].astype(f32) * line_ref[0:1, :]
+        start_cos, start_sin = jnp.cos(start), jnp.sin(start)
+        signs = line_ref[1:2, :]
+        cos_at[p] = cos_ref[...] * start_cos - sin_ref[...] * (start_sin * signs)
+        sin_at[p] = sin_ref[...] * start_cos + cos_ref[...] * (start_sin * signs)
     gather(to_tensor, sq, me, 0, n_t - 1)
     gather(to_tensor, sqd, me, 1, n_t - 1)
 
@@ -217,14 +235,14 @@
             lanes = pl.ds(j * LANES, LANES)
             for p in range(prompts):
                 part = acc[pl.ds(p * PLEN, PLEN), lanes]
-                kbuf[k, p, j] = rotated(part, cos_ref[p], sin_ref[p]).astype(bf16)
+                kbuf[k, p, j] = rotated(part, cos_at[p], sin_at[p]).astype(bf16)
             d_send[k, 0, j] = acc[pl.ds(tokens, pad), lanes]
 
     each(n_t, keys)
 
     gathered(to_shard, q1, shard, 0, n_s - 1, n_s)
     for p in range(prompts):
-        owner = owner_ref[p]
+        owner = owners[p]
         q2[me, p] = q1[owner // rows, lax.rem(owner, rows)]
     gather(to_tensor, q2, me, 2, n_t - 1)
     gathered(to_tensor, q2, me, 2, n_t - 1, n_t)
@@ -276,7 +294,7 @@
                     contract_last,
                     preferred_element_type=f32,
                 )
-                mask = position < length_ref[r]
+                mask = position < row_lengths[r]
                 found = jnp.where(mask, found * scale, very_negative)
                 top = jnp.max(found, axis=1, keepdims=True)
                 weights = jnp.where(mask, jnp.exp(found - top), 0.0)
@@ -364,6 +382,13 @@
     own_row = lax.broadcasted_iota(jnp.int32, (unit_rows, pad), 0)
     column = lax.broadcasted_iota(jnp.int32, (unit_rows, pad), 1)
     causal = (column // rows <= own_row // unit) & (column < steps * rows)
+    spot = lax.broadcasted_iota(jnp.int32, (pad, LANES), 0)
+    place = jnp.zeros((pad, LANES), jnp.int32)
+    for r in range(rows):
+        start = row_lengths[r] + PLEN * row_new[r]
+        place = jnp.where(lax.rem(spot, rows) == r, start + spot // rows, place)
+    angles = place.astype(f32) * line_ref[0:1, :]
+    step_cos, step_sin = jnp.cos(angles), jnp.sin(angles) * line_ref[1:2, :]
     states = {}
     for j in range(kpc):
         terms = []
@@ -372,7 +397,7 @@
             for k in range(n_t - 1):
                 total += d_recv[k, value, j]
             terms.append(total * factor)
-        key = rotated(terms[0], step_cos_ref[...], step_sin_ref[...]).astype(bf16)
+        key = rotated(terms[0], step_cos, step_sin).astype(bf16)
         value = terms[1].astype(bf16)
         for r in range(rows):
             found = lax.dot_general(
@@ -404,14 +429,20 @@
     for j in range(kpc):
         for r in range(rows):
             top, whole, mixed = states[j, r]
-            pick = pick_ref[r]
+            pick = row_pick[r]
             source, p = pick // prompts, lax.rem(pick, prompts)
             log = lse_all[source, p, j]
-            log = jnp.where(new_ref[r] > 0, log, very_negative)
+            log = jnp.where(row_new[r] > 0, log, very_negative)
             out = o_all[source, p, j].astype(f32)
             last = jnp.maximum(top, log)
             left, right = jnp.exp(top - last), jnp.exp(log - last)
-            out_ref[r, j] = ((mixed * left + out * right) / (whole * left + right)).astype(bf16)
+            out = (mixed * left + out * right) / (whole * left + right)
+            for step in range(steps):
+                for h in range(unit):
+                    lanes = pl.ds((j * unit + h) * LANES, LANES)
+                    at = step * unit + h
+                    out_wide[step, r : r + 1, lanes] = out[at : at + 1, :]
+    out_ref[...] = out_wide[...].astype(bf16)
 
     sent(to_shard, q1, shard, 0, n_s - 1)
     sent(to_shard, lse_all, shard, 1, n_s - 1)
@@ -437,7 +468,6 @@
     n_t = lax.axis_size("tensor")
     n_s = lax.axis_size(shards)
     n_seq = lax.axis_size("seq")
-    shard_rank = lax.axis_index(shards)
     tokens, features = prompt_hidden.shape
     steps, rows, query_width = queries.shape
     kv_heads, cache_rows = kv_cache.shape[1:3]
@@ -452,25 +482,7 @@
     pad = -(-steps * rows // 16) * 16
     cols = kpc * head_size
 
-    my_owners = lax.dynamic_slice_in_dim(prompt_row, shard_rank * prompts, prompts, 0)
-    my_rows = shard_rank * rows + jnp.arange(rows, dtype=jnp.int32)
-    my_lengths = lax.dynamic_slice_in_dim(lengths, shard_rank * rows, rows, 0)
-    owned = prompt_row[None, :] == my_rows[:, None]
-    is_new = jnp.any(owned, axis=1).astype(jnp.int32)
-    pick = jnp.sum(
-        jnp.where(owned, jnp.arange(prompt_row.shape[0], dtype=jnp.int32)[None, :], 0), axis=1
-    )
-    positions = (
-        jnp.take(lengths, my_owners)[:, None] + jnp.arange(PLEN, dtype=jnp.int32)[None, :]
-    )
-    cosine, sine_part = angle_tables(positions, head_size)
-    step_ids = jnp.arange(steps, dtype=jnp.int32)
-    step_pos = (my_lengths + PLEN * is_new)[None, :] + step_ids[:, None]
-    step_pos = jnp.pad(step_pos.reshape(-1), (0, pad - steps * rows))
-    step_cos, step_sin = angle_tables(step_pos, head_size)
-    step_hidden = jnp.pad(
-        decode_hidden.reshape(steps * rows, features), ((0, pad - steps * rows), (0, 0))
-    )
+    cosine, sine_part, line = angle_tables(head_size)
     query_units = jnp.transpose(
         queries.reshape(steps, rows, n_t, kpc, unit, head_size), (2, 1, 3, 0, 4, 5)
     ).reshape(n_t, rows, kpc, unit_rows, head_size)
@@ -481,11 +493,11 @@
     per_unit = (kpc, unit_rows)
     dma = pltpu.SemaphoreType.DMA
     flops = 2 * tokens * features * 2 * cols * n_t
-    result = pl.pallas_call(
+    return pl.pallas_call(
         functools.partial(kernel, (n_t, n_s, n_seq, kpc, unit, group, steps, rows)),
-        out_shape=jax.ShapeDtypeStruct((rows,) + per_unit + (head_size,), bf16),
-        in_specs=[hbm, vmem, vmem, hbm, hbm, vmem, vmem, vmem, vmem, vmem]
-        + [smem, smem, smem, smem],
+        out_shape=jax.ShapeDtypeStruct((steps, rows, local_heads * head_size), bf16),
+        in_specs=[hbm, vmem, vmem, hbm, hbm, vmem, vmem, vmem, vmem]
+        + [smem, smem],
         out_specs=vmem,
         scratch_shapes=[
             pltpu.VMEM((tokens + pad, features), bf16),
@@ -513,6 +525,9 @@
             pltpu.VMEM((n_t - 1,) + per_unit + (LANES,), f32),
             pltpu.VMEM((n_t, 2, kpc, pad, head_size), f32),
             pltpu.VMEM((n_t - 1, 2, kpc, pad, head_size), f32),
+            pltpu.VMEM((prompts, PLEN, head_size), f32),
+            pltpu.VMEM((prompts, PLEN, head_size), f32),
+            pltpu.VMEM((steps, rows, local_heads * head_size), f32),
             dma((tokens // BLOCK,)),
             dma((2, kpc, n_t)),
             dma,
@@ -527,22 +542,17 @@
         ),
     )(
         prompt_hidden,
-        step_hidden,
+        decode_hidden,
         norm_gain.reshape(1, features),
         kv_weight,
         kv_cache,
         query_units,
         cosine,
         sine_part,
-        step_cos,
-        step_sin,
-        my_owners,
-        my_lengths,
-        is_new,
-        pick,
+        line,
+        lengths,
+        prompt_row,
     )
-    result = result.reshape(rows, kpc, steps, unit, head_size)
-    return jnp.transpose(result, (2, 0, 1, 3, 4)).reshape(steps, rows, local_heads * head_size)
 
 
 def solution(mesh):

time: 83.7 us -> 70.7 us (0.84)
  other arithmetic: 10.2 us -> 0 us
  local copies, waits for them, and re-layouts: 7.66 us -> 4.74 us
    neg x2 -> x0, other arithmetic: 2.94 us -> none  [angle_tables(): -sine_part]
    concatenate x2 -> x0, other arithmetic: 2.32 us -> none  [angle_tables(): jnp.concatenate([cosine, cosine], -1)]
    reshape x2 -> x0, local copies, waits for them, and re-layouts: 1.46 us -> none  [the longest x1 0.81 us: per_device(): decode_hidden.reshape(steps * rows, features)]
    unnamed x2 -> x1, local copies, waits for them, and re-layouts: 0.01 us -> 1.44 us
    reduce_sum x1 -> x0, other arithmetic: 1.41 us -> none  [per_device(): jnp.sum(jnp.where(owned, jnp.arange(prompt_row.shape[0], dtype=jnp.int32)...]
    add x3 -> x0, other arithmetic: 1.31 us -> none  [the longest x2 1.31 us: per_device(): step_pos = (my_lengths + PLEN * is_new)[None, :] + step_ids[:, None]]
    gather x1 -> x0, local copies, waits for them, and re-layouts: 1.29 us -> none  [per_device(): jnp.take(lengths, my_owners)[:, None]]
    pallas_call x1 -> x0, local copies, waits for them, and re-layouts: 0.84 us -> none  [per_device(): pl.pallas_call(functools.partial(kernel, (n_t, n_s, n_seq, kpc, unit, gro...]
where the time goes in v3:
time: 70.7 us; the launch traced here: 70.4 us
  Pallas kernels  65.7 us (93%)
  local copies, waits for them, and re-layouts  4.74 us (7%)
    pallas_call x1, Pallas kernels, per_device(): pl.pallas_call(functools.partial(kernel, (n_t, n_s, n_seq, kpc, unit, gro...  65.7 us
    unnamed x1, local copies, waits for them, and re-layouts  1.44 us

profile of v3, /device:TPU:0, one launch (start us, length us, event | category | flops | bytes accessed | tf_op | source)
XLA Modules:
  0.0 70.4 jit_solution(17758804353223613225)
XLA Ops:
  0.0 1.2 %reshape.10 = bf16[2,4,4,2,12,128]{5,4,3,2,1,0:T(8,128)(2,1)S(1)} reshape(bf16[2,4,12288]{2,1,0:T(4,128)(2,1)} %param.16) | data formatting | bytes 393216 | tf_op jit(solution)/shard_map/reshape | solution.py:487
  1.2 0.2 copy.13
  1.3 0.7 copy.14.query_ref
  2.0 1.3 %reshape.9.gain_ref = bf16[1,3072]{1,0:T(2,128)(2,1)} reshape(bf16[3072]{0:T(1024)(128)(2,1)} %param.13) | data formatting | bytes 12288 | tf_op jit(solution)/shard_map/reshape | solution.py:546
  3.3 65.7 %shard_map.109 = bf16[2,4,3072]{2,1,0:T(4,128)(2,1)} custom-call(bf16[1536,3072]{1,0:T(8,128)(2,1)} %prompt_ref.1, bf16[2,4,3072]{2,1,0:T(4,128)(2,1)} %step_hidden_ref.1, bf16[1,3072]{1,0:T(2,128)(2,1)} %reshape.9.gain_ref, bf16[3072,2048]{1,0:T(8,128)(2,1)} %weight_ref.1, bf16[4,8,256,256]{3,2,1,0:T(8,128)(2,1)} %cache_ref.1, ...), custom_call_target="tpu_custom_call" | custom-call | flops 19327352832 | bytes 30000000 | tf_op jit(solution)/shard_map/pallas_call | solution.py:496
  69.0 1.4 %copy.16 = bf16[2,4,3072]{2,1,0:T(4,128)(2,1)} copy(bf16[2,4,3072]{2,1,0:T(4,128)(2,1)} %shard_map.109) | data formatting | bytes 98304

commit v4 on v3

--- a/solution.py
+++ b/solution.py
@@ -80,6 +80,7 @@
     cos_at,
     sin_at,
     out_wide,
+    s_own,
     x_sem,
     w_sem,
     c_sem,
@@ -158,11 +159,11 @@
         )
 
     c_copy = pltpu.make_async_copy(cache_ref, cbuf, c_sem)
+    c_copy.start()
     each(blocks, lambda b: x_copy(b).start())
     for value in range(2):
         for j in range(kpc):
             each(n_t, lambda k: w_copy(k, j, value).start())
-    c_copy.start()
 
     barrier = pltpu.get_barrier_semaphore()
 
@@ -197,85 +198,6 @@
 
     q1[shard] = query_ref[me]
     gather(to_shard, q1, shard, 0, n_s - 1)
-
-    def weigh(b):
-        x_copy(b).wait()
-        at = pl.ds(pl.multiple_of(b * BLOCK, BLOCK), BLOCK)
-        square = jnp.zeros((BLOCK, LANES), f32)
-        for c in range(features // LANES):
-            lanes = pl.ds(c * LANES, LANES)
-            wide = xw[at, lanes].astype(f32)
-            square += wide * wide
-            xw[at, lanes] = (wide * gain_ref[:, lanes].astype(f32)).astype(bf16)
-        total = jnp.sum(square.T, axis=0, keepdims=True)
-        sq[me, b] = jnp.broadcast_to(total, (8, BLOCK))
-
-    each(blocks, weigh)
-    wide = [step_hidden_ref[step].astype(f32) for step in range(steps)]
-    wide.append(jnp.zeros((pad - steps * rows, features), f32))
-    wide = jnp.concatenate(wide, axis=0)
-    sqd[me] = jnp.broadcast_to(
-        jnp.sum(wide * wide, axis=1, keepdims=True), (pad, LANES)
-    )
-    xw[pl.ds(tokens, pad), :] = (wide * gain_ref[...].astype(f32)).astype(bf16)
-    for p in range(prompts):
-        start = length_ref[owners[p]].astype(f32) * line_ref[0:1, :]
-        start_cos, start_sin = jnp.cos(start), jnp.sin(start)
-        signs = line_ref[1:2, :]
-        cos_at[p] = cos_ref[...] * start_cos - sin_ref[...] * (start_sin * signs)
-        sin_at[p] = sin_ref[...] * start_cos + cos_ref[...] * (start_sin * signs)
-    gather(to_tensor, sq, me, 0, n_t - 1)
-    gather(to_tensor, sqd, me, 1, n_t - 1)
-
-    def keys(k):
-        for j in range(kpc):
-            w_copy(k, j, 0).wait()
-        acc[...] = jnp.dot(xw[...], wk[k], preferred_element_type=f32)
-        for j in range(kpc):
-            lanes = pl.ds(j * LANES, LANES)
-            for p in range(prompts):
-                part = acc[pl.ds(p * PLEN, PLEN), lanes]
-                kbuf[k, p, j] = rotated(part, cos_at[p], sin_at[p]).astype(bf16)
-            d_send[k, 0, j] = acc[pl.ds(tokens, pad), lanes]
-
-    each(n_t, keys)
-
-    gathered(to_shard, q1, shard, 0, n_s - 1, n_s)
-    for p in range(prompts):
-        owner = owners[p]
-        q2[me, p] = q1[owner // rows, lax.rem(owner, rows)]
-    gather(to_tensor, q2, me, 2, n_t - 1)
-    gathered(to_tensor, q2, me, 2, n_t - 1, n_t)
-
-    def score(k):
-        t = chunk(k)
-        for p in range(prompts):
-            for j in range(kpc):
-                s_send[k, p, j] = lax.dot_general(
-                    q2[t, p, j], kbuf[k, p, j], contract_last, preferred_element_type=f32
-                )
-
-        @pl.when(k < n_t - 1)
-        def _():
-            to_tensor(s_send.at[k], s_recv.at[k], 3, k).start()
-
-    each(n_t, score)
-
-    def values(k):
-        for j in range(kpc):
-            w_copy(k, j, 1).wait()
-        acc[...] = jnp.dot(xw[...], wv[k], preferred_element_type=f32)
-        for j in range(kpc):
-            lanes = pl.ds(j * LANES, LANES)
-            for p in range(prompts):
-                vbuf[k, p, j] = acc[pl.ds(p * PLEN, PLEN), lanes].astype(bf16)
-            d_send[k, 1, j] = acc[pl.ds(tokens, pad), lanes]
-
-        @pl.when(k < n_t - 1)
-        def _():
-            to_tensor(d_send.at[k], d_recv.at[k], 4, k).start()
-
-    each(n_t, values)
 
     c_copy.wait()
     position = me * cache_rows + lax.broadcasted_iota(jnp.int32, (unit_rows, cache_rows), 1)
@@ -319,6 +241,98 @@
 
     each(n_t, resident)
 
+
+    gains = [gain_ref[pl.ds(c * LANES, LANES)][None, :] for c in range(features // LANES)]
+
+    def weigh(b):
+        x_copy(b).wait()
+        at = pl.ds(pl.multiple_of(b * BLOCK, BLOCK), BLOCK)
+        square = jnp.zeros((BLOCK, LANES), f32)
+        for c in range(features // LANES):
+            lanes = pl.ds(c * LANES, LANES)
+            part = xw[at, lanes]
+            wide = part.astype(f32)
+            square += wide * wide
+            xw[at, lanes] = part * gains[c]
+        total = jnp.sum(square.T, axis=0, keepdims=True)
+        sq[me, b] = jnp.broadcast_to(total, (8, BLOCK))
+
+    each(blocks, weigh)
+    wide = [step_hidden_ref[step].astype(f32) for step in range(steps)]
+    wide.append(jnp.zeros((pad - steps * rows, features), f32))
+    wide = jnp.concatenate(wide, axis=0)
+    sqd[me] = jnp.broadcast_to(
+        jnp.sum(wide * wide, axis=1, keepdims=True), (pad, LANES)
+    )
+    xw[pl.ds(tokens, pad), :] = (wide * gain_ref[...].astype(f32)[None, :]).astype(bf16)
+    for p in range(prompts):
+        start = length_ref[owners[p]].astype(f32) * line_ref[0:1, :]
+        start_cos, start_sin = jnp.cos(start), jnp.sin(start)
+        signs = line_ref[1:2, :]
+        cos_at[p] = cos_ref[...] * start_cos - sin_ref[...] * (start_sin * signs)
+        sin_at[p] = sin_ref[...] * start_cos + cos_ref[...] * (start_sin * signs)
+    gather(to_tensor, sq, me, 0, n_t - 1)
+    gather(to_tensor, sqd, me, 1, n_t - 1)
+
+    def keys(k):
+        for j in range(kpc):
+            w_copy(k, j, 0).wait()
+        acc[...] = jnp.dot(xw[...], wk[k], preferred_element_type=f32)
+        for j in range(kpc):
+            lanes = pl.ds(j * LANES, LANES)
+            for p in range(prompts):
+                part = acc[pl.ds(p * PLEN, PLEN), lanes]
+                kbuf[k, p, j] = rotated(part, cos_at[p], sin_at[p]).astype(bf16)
+            d_send[k, 0, j] = acc[pl.ds(tokens, pad), lanes]
+
+    early = n_t // 2
+    each(early, keys)
+
+    gathered(to_shard, q1, shard, 0, n_s - 1, n_s)
+    for p in range(prompts):
+        owner = owners[p]
+        q2[me, p] = q1[owner // rows, lax.rem(owner, rows)]
+    gather(to_tensor, q2, me, 2, n_t - 1)
+    gathered(to_tensor, q2, me, 2, n_t - 1, n_t)
+
+    def score(k):
+        t = chunk(k)
+        for p in range(prompts):
+            for j in range(kpc):
+                part = lax.dot_general(
+                    q2[t, p, j], kbuf[k, p, j], contract_last, preferred_element_type=f32
+                )
+                s_own[p, j] = part
+                s_send[k, p, j] = part.astype(bf16)
+
+        @pl.when(k < n_t - 1)
+        def _():
+            to_tensor(s_send.at[k], s_recv.at[k], 3, k).start()
+
+    each(early, score)
+
+    def late(k):
+        keys(k + early)
+        score(k + early)
+
+    each(n_t - early, late)
+
+    def values(k):
+        for j in range(kpc):
+            w_copy(k, j, 1).wait()
+        acc[...] = jnp.dot(xw[...], wv[k], preferred_element_type=f32)
+        for j in range(kpc):
+            lanes = pl.ds(j * LANES, LANES)
+            for p in range(prompts):
+                vbuf[k, p, j] = acc[pl.ds(p * PLEN, PLEN), lanes].astype(bf16)
+            d_send[k, 1, j] = acc[pl.ds(tokens, pad), lanes]
+
+        @pl.when(k < n_t - 1)
+        def _():
+            to_tensor(d_send.at[k], d_recv.at[k], 4, k).start()
+
+    each(n_t, values)
+
     gathered(to_tensor, sq, me, 0, n_t - 1, n_t)
     gathered(to_tensor, sqd, me, 1, n_t - 1, n_t)
     each(n_t - 1, lambda k: to_tensor(s_send.at[k], s_recv.at[k], 3, k).wait_recv())
@@ -332,9 +346,9 @@
             parts.append(lax.rsqrt(total[0:1] / D + epsilon))
         factor = jnp.concatenate(parts, axis=1)
         for j in range(kpc):
-            total = s_send[n_t - 1, p, j]
+            total = s_own[p, j]
             for k in range(n_t - 1):
-                total += s_recv[k, p, j]
+                total += s_recv[k, p, j].astype(f32)
             total = total * (factor * scale)
             top = jnp.max(total, axis=1, keepdims=True)
             weights = jnp.exp(total - top)
@@ -511,8 +525,8 @@
             pltpu.VMEM((n_t, prompts) + per_unit + (head_size,), bf16),
             pltpu.VMEM((n_t, tokens // BLOCK, 8, BLOCK), f32),
             pltpu.VMEM((n_t, pad, LANES), f32),
-            pltpu.VMEM((n_t, prompts) + per_unit + (PLEN,), f32),
-            pltpu.VMEM((n_t - 1, prompts) + per_unit + (PLEN,), f32),
+            pltpu.VMEM((n_t, prompts) + per_unit + (PLEN,), bf16),
+            pltpu.VMEM((n_t - 1, prompts) + per_unit + (PLEN,), bf16),
             pltpu.VMEM((n_t, prompts) + per_unit + (PLEN,), bf16),
             pltpu.VMEM((n_s, prompts) + per_unit + (LANES,), f32),
             pltpu.VMEM((prompts,) + per_unit + (LANES,), f32),
@@ -528,6 +542,7 @@
             pltpu.VMEM((prompts, PLEN, head_size), f32),
             pltpu.VMEM((prompts, PLEN, head_size), f32),
             pltpu.VMEM((steps, rows, local_heads * head_size), f32),
+            pltpu.VMEM((prompts,) + per_unit + (PLEN,), f32),
             dma((tokens // BLOCK,)),
             dma((2, kpc, n_t)),
             dma,
@@ -543,7 +558,7 @@
     )(
         prompt_hidden,
         decode_hidden,
-        norm_gain.reshape(1, features),
+        norm_gain,
         kv_weight,
         kv_cache,
         query_units,

time: 70.7 us -> 69.8 us (0.987)
  local copies, waits for them, and re-layouts: 4.74 us -> 3.44 us
    reshape x1 -> x0, local copies, waits for them, and re-layouts: 1.3 us -> none  [per_device(): norm_gain.reshape(1, features)]
where the time goes in v4:
time: 69.8 us; the launch traced here: 69.6 us
  Pallas kernels  66.1 us (95%)
  local copies, waits for them, and re-layouts  3.44 us (5%)
    pallas_call x1, Pallas kernels, per_device(): pl.pallas_call(functools.partial(kernel, (n_t, n_s, n_seq, kpc, unit, gro...  66.1 us
    unnamed x1, local copies, waits for them, and re-layouts  1.44 us

profile of v4, /device:TPU:0, one launch (start us, length us, event | category | flops | bytes accessed | tf_op | source)
XLA Modules:
  0.0 69.6 jit_solution(18272572366051283429)
XLA Ops:
  0.0 1.2 %reshape.6 = bf16[2,4,4,2,12,128]{5,4,3,2,1,0:T(8,128)(2,1)S(1)} reshape(bf16[2,4,12288]{2,1,0:T(4,128)(2,1)} %param.16) | data formatting | bytes 393216 | tf_op jit(solution)/shard_map/reshape | solution.py:501
  1.2 0.2 copy.13
  1.3 0.7 %copy.14.query_ref = bf16[4,4,2,24,128]{4,3,2,1,0:T(8,128)(2,1)} copy(bf16[4,4,2,24,128]{4,2,3,1,0:T(2,128)(2,1)S(1)} %bitcast.3) | data formatting | bytes 393216 | tf_op jit(solution)/shard_map/reshape | solution.py:502
  2.0 66.1 %shard_map.109 = bf16[2,4,3072]{2,1,0:T(4,128)(2,1)} custom-call(bf16[1536,3072]{1,0:T(8,128)(2,1)} %prompt_ref.1, bf16[2,4,3072]{2,1,0:T(4,128)(2,1)} %step_hidden_ref.1, bf16[3072]{0:T(1024)(128)(2,1)} %gain_ref.1, bf16[3072,2048]{1,0:T(8,128)(2,1)} %weight_ref.1, bf16[4,8,256,256]{3,2,1,0:T(8,128)(2,1)} %cache_ref.1, ...), custom_call_target="tpu_custom_call" | custom-call | flops 19327352832 | bytes 30000000 | tf_op jit(solution)/shard_map/pallas_call | solution.py:510
  68.1 1.4 %copy.16 = bf16[2,4,3072]{2,1,0:T(4,128)(2,1)} copy(bf16[2,4,3072]{2,1,0:T(4,128)(2,1)} %shard_map.109) | data formatting | bytes 98304
